TPU v7x, 512 devices: a whole 4x4x16 slice. The times are simulated.
512 devices in a mesh: phase: 2 (over core), dp: 256 (over z, x, y).
Axes of the slice: x: 4, y: 4, z: 16, core: 2. Of those that a mesh axis runs over, the one named last changes fastest.
Arguments:
- tokens: bfloat16 [2, 24576, 1280], P(None, 'dp'), may hold values from -6 to 6
- segment_ids: int32 [2, 24576], replicated, may hold values from 0 to 3, as said below
- loss_mask: int32 [2, 24576], P(None, 'dp'), may hold values 0 or 1
- qkv_weight: bfloat16 [2, 1280, 3840], P('phase', 'dp'), may hold values from -0.15625 to 0.15625
- gains: float32 [2, 1280], P('phase'), may hold values from 0.5 to 1.5
- cotangent: bfloat16 [2, 24576, 1280], P(None, 'dp'), may hold values from -24 to 24
Outputs:
- boundary: bfloat16 [2, 2, 24576, 1280], P('phase', None, 'dp')
- gain_grad: float32 [2, 1280], P('phase', 'dp')
Inputs may be any that keep to these rules, and one draw needn't show every extreme that they name: `segment_ids`: in each micro-batch the label is 0 at the first token and moves on by one, modulo 4, at the first token of each MSA sequence; it never changes elsewhere.
All inputs are finite; a program needn't handle non-finite values. No bound on the sum of `loss_mask` on one device may be relied on, other than what follows from the above.
Results may differ from a plain program's by a relative error of at most 0.014.
Values may be sent and summed in bfloat16 or wider, within the bound.
A program may use at most 128 MiB of HBM per device.

v0:
```python
import math

import jax
import jax.numpy as jnp
from jax import lax
from jax.sharding import PartitionSpec as P

WIDTH = 1280
HEADS = 16
HEAD_DIM = 80


def passed_along(x, axis, by):
    size = lax.axis_size(axis)
    pairs = [(i, i + by) for i in range(size) if 0 <= i + by < size]
    return lax.ppermute(x, axis, pairs)


def normalize(inputs, scaling):
    widened = inputs.astype(jnp.float32)
    inverse = lax.rsqrt(jnp.mean(widened * widened, axis=-1, keepdims=True) + 1e-05)
    normed = (widened * inverse * scaling).astype(jnp.bfloat16)
    return (widened, inverse, normed)


def split_project(project, remote_pair):
    length = project.shape[0]
    local = project.reshape(length, 3, HEADS, HEAD_DIM).astype(jnp.float32)
    remote = remote_pair.reshape(length, 2, HEADS, HEAD_DIM).astype(jnp.float32)
    queries = local[:, 0]
    key_rows = jnp.concatenate([remote[:, 0], local[:, 1]], axis=0)
    values = jnp.concatenate([remote[:, 1], local[:, 2]], axis=0)
    return (queries, key_rows, values)


def allowed_keys(seg_local, seg_remote, has_left):
    length = seg_local.shape[0]
    position = jnp.arange(length)
    local_ok = (seg_local[:, None] == seg_local[None, :]) & (position[None, :] <= position[:, None])
    remote_ok = (seg_local[:, None] == seg_remote[None, :]) & has_left
    return jnp.concatenate([remote_ok, local_ok], axis=1)


def probabilities(queries, key_rows, allowed):
    scores = jnp.einsum("qhd,khd->hqk", queries, key_rows) / math.sqrt(HEAD_DIM)
    scores = jnp.where(allowed[None], scores, -1e30)
    highest = jnp.max(scores, axis=-1, keepdims=True)
    exponent = jnp.exp(scores - highest)
    return exponent / jnp.sum(exponent, axis=-1, keepdims=True)


def shards(tokens, segment_ids, loss_mask, qkv_weight, gains, cotangent):
    micro_count = tokens.shape[0]
    rows = tokens.shape[1]
    first = lax.axis_index("phase") == 0
    place = lax.axis_index("dp")
    has_left = place > 0
    scaling = gains[0]
    masks = []
    for micro_index in range(micro_count):
        seg_row = segment_ids[micro_index]
        seg_local = lax.dynamic_slice_in_dim(seg_row, place * rows, rows)
        seg_remote = lax.dynamic_slice_in_dim(seg_row, jnp.maximum(place - 1, 0) * rows, rows)
        masks.append(allowed_keys(seg_local, seg_remote, has_left))
    incoming = jnp.zeros_like(tokens[0])
    weight = None
    inputs_seen = []
    allowed_seen = []
    records = []
    outputs_seen = []
    for tick in range(micro_count + 1):
        early = min(tick, micro_count - 1)
        later = max(tick - 1, 0)
        allowed = jnp.where(first, masks[early], masks[later])
        entering = jnp.where(first, tokens[early], incoming)
        widened, inverse, normed = normalize(entering, scaling)
        if tick == 0:
            weight = lax.all_gather(qkv_weight, "dp", axis=1, tiled=True)[0]
            project = jnp.dot(normed, weight, preferred_element_type=jnp.float32).astype(
                jnp.bfloat16
            )
        else:
            project = jnp.dot(normed, weight, preferred_element_type=jnp.float32).astype(
                jnp.bfloat16
            )
        remote_pair = passed_along(project[:, WIDTH:], "dp", 1)
        queries, key_rows, values = split_project(project, remote_pair)
        softmax = probabilities(queries, key_rows, allowed)
        rounded = lax.optimization_barrier(softmax.astype(jnp.bfloat16)).astype(jnp.float32)
        attended = jnp.einsum("hqk,khd->qhd", rounded, values)
        result = (widened + attended.reshape(rows, WIDTH)).astype(jnp.bfloat16)
        inputs_seen.append(entering)
        allowed_seen.append(allowed)
        records.append((inverse, project, remote_pair, softmax))
        outputs_seen.append(result)
        if tick < micro_count:
            incoming = passed_along(result, "phase", 1)
    received = jnp.zeros_like(tokens[0])
    gain_local = jnp.zeros((WIDTH,), jnp.float32)
    grads_out = [received] * micro_count
    for step_index in range(micro_count + 1):
        tick = micro_count - step_index
        later = max(micro_count - 1 - step_index, 0)
        selected = loss_mask[later][:, None] == 1
        upstream_top = jnp.where(selected, cotangent[later], jnp.zeros((), jnp.bfloat16))
        upstream = jnp.where(first, received, upstream_top)
        inverse, project, remote_pair, softmax = records[tick]
        queries, key_rows, values = split_project(project, remote_pair)
        rounded = lax.optimization_barrier(softmax.astype(jnp.bfloat16)).astype(jnp.float32)
        widened = inputs_seen[tick].astype(jnp.float32)
        flowing = upstream.astype(jnp.float32)
        per_head = flowing.reshape(rows, HEADS, HEAD_DIM)
        grad_soft = jnp.einsum("qhd,khd->hqk", per_head, values)
        grad_values = jnp.einsum("hqk,qhd->khd", rounded, per_head)
        grad_scores = (
            softmax
            * (grad_soft - jnp.sum(softmax * grad_soft, axis=-1, keepdims=True))
            / math.sqrt(HEAD_DIM)
        )
        grad_queries = jnp.einsum("hqk,khd->qhd", grad_scores, key_rows)
        grad_keys = jnp.einsum("hqk,qhd->khd", grad_scores, queries)
        remote_grad = jnp.concatenate(
            [grad_keys[:rows].reshape(rows, WIDTH), grad_values[:rows].reshape(rows, WIDTH)], axis=1
        )
        returned = passed_along(remote_grad.astype(jnp.bfloat16), "dp", -1).astype(
            remote_grad.dtype
        )
        own_keys = grad_keys[rows:].reshape(rows, WIDTH) + returned[:, :WIDTH]
        own_values = grad_values[rows:].reshape(rows, WIDTH) + returned[:, WIDTH:]
        grad_project = jnp.concatenate(
            [grad_queries.reshape(rows, WIDTH), own_keys, own_values], axis=1
        ).astype(jnp.bfloat16)
        grad_normed = jnp.dot(grad_project, weight.T, preferred_element_type=jnp.float32)
        grad_gain = jnp.sum(grad_normed * widened * inverse, axis=0)
        scaled = grad_normed * scaling
        grad_inputs = inverse * (
            scaled
            - widened * inverse * inverse * jnp.mean(scaled * widened, axis=-1, keepdims=True)
        )
        grad_inputs = (flowing + grad_inputs).astype(jnp.bfloat16)
        useful = jnp.where(first, step_index > 0, step_index < micro_count)
        masked = jnp.where(useful, grad_gain, jnp.zeros((), jnp.float32))
        gain_local = gain_local + masked
        if step_index > 0:
            grads_out[tick] = grad_inputs
        if step_index < micro_count:
            received = passed_along(grad_inputs, "phase", -1)
    forward_stack = jnp.stack(outputs_seen[1:])
    backward_stack = jnp.stack(grads_out)
    boundary = jnp.where(first, backward_stack, forward_stack)[None]
    gain_grad = lax.psum_scatter(gain_local[None], "dp", scatter_dimension=1, tiled=True)
    return (boundary, gain_grad)


def solution(mesh):
    in_specs = (
        P(None, "dp", None),
        P(),
        P(None, "dp"),
        P("phase", "dp", None),
        P("phase", None),
        P(None, "dp", None),
    )
    out_specs = (P("phase", None, "dp", None), P("phase", "dp"))
    return jax.shard_map(shards, mesh=mesh, in_specs=in_specs, out_specs=out_specs, check_vma=False)
```

profile of v0, /device:TPU:128, one launch (start us, length us, event | category | flops | bytes accessed | tf_op | source)
XLA Modules:
  0.0 1205.9 jit_solution(16928899103045248610)
XLA Ops:
  11.9 245.3 %all-gather.2.cloned.1.call-done = bf16[1,1280,3840]{2,0,1:T(2,128)(2,1)} async-done(((bf16[1,5,3840]{2,0,1:T(2,128)(2,1)}), bf16[1,1280,3840]{2,0,1:T(2,128)(2,1)}) %all-gather.2.cloned.1.call-update) | async-done | bytes 9830416 | tf_op jit(solution)/shard_map/all_gather | solution.py:78
  257.2 10.2 copy.98
  271.2 3.2 collective-permute-start
  276.0 13.4 %collective-permute-done = bf16[96,2560]{1,0:T(8,128)(2,1)S(1)} collective-permute-done((bf16[96,2560]{1,0:T(8,128)(2,1)S(1)}, bf16[96,2560]{1,0:T(8,128)(2,1)S(1)}, u32[]{:S(2)}, u32[]{:S(2)}) %collective-permute-start) | collective-permute-done | bytes 491552 | tf_op jit(solution)/shard_map/ppermute | solution.py:16
  290.6 3.2 fusion.164
  298.8 5.6 fusion.18
  308.7 17.6 %collective-permute-done.2 = bf16[96,2560]{1,0:T(8,128)(2,1)} collective-permute-done((bf16[96,2560]{1,0:T(8,128)(2,1)}, bf16[96,2560]{1,0:T(8,128)(2,1)}, u32[]{:S(2)}, u32[]{:S(2)}) %collective-permute-start.2) | collective-permute-done | bytes 491552 | tf_op jit(solution)/shard_map/ppermute | solution.py:16
  328.6 3.1 fusion.165
  337.5 5.6 fusion.21
  350.4 14.7 %collective-permute-done.4 = bf16[96,2560]{1,0:T(8,128)(2,1)} collective-permute-done((bf16[96,2560]{1,0:T(8,128)(2,1)}, bf16[96,2560]{1,0:T(8,128)(2,1)}, u32[]{:S(2)}, u32[]{:S(2)}) %collective-permute-start.4) | collective-permute-done | bytes 491552 | tf_op jit(solution)/shard_map/ppermute | solution.py:16
  367.3 3.6 fusion.166
  370.9 3.7 multiply_reduce_fusion.2
  378.7 2.7 convolution_bitcast_fusion.2
  387.1 2.0 collective-permute-start.5
  389.1 2.3 fusion.30
  394.7 2.2 copy.80
  397.8 3.5 convolution_convert_fusion.2
  405.4 7.1 fusion.94
  417.1 4.0 multiply_reduce_fusion.1
  422.8 2.7 convolution_bitcast_fusion.1
  429.2 6.4 collective-permute-start.7
  439.6 2.9 convolution_convert_fusion.1
  442.6 4.1 collective-permute-done.7
  448.5 7.1 fusion.89
  457.2 2.1 collective-permute-done.8
  459.6 3.5 multiply_reduce_fusion
  463.7 2.7 convolution_bitcast_fusion
  468.4 9.8 collective-permute-start.9
  483.0 2.7 convolution_convert_fusion
  485.8 3.4 collective-permute-done.9
  491.1 7.1 fusion.82
  498.2 699.2 %all-reduce = f32[1,1280]{1,0:T(1,128)S(1)} all-reduce(f32[1,1280]{1,0:T(1,128)S(1)} %add.114), channel_id=2, replica_groups=mesh['phase'=2,'dp'=256] {'dp'}, use_global_device_ids=true, to_apply=%region_18.19.clone | all-reduce | flops 1280 | bytes 10240
  (228 shorter events, 83.9 us)
Async XLA Ops:
  7.2 250.0 %all-gather.2.cloned.1.call-start = ((), (), s32[]{:S(2)}) async-start(), calls=%async_computation | async-start | bytes 19737600 | tf_op jit(solution)/shard_map/all_gather | solution.py:78
  11.9 255.5 %copy-start.46 = (f32[96]{0:T(128)}, f32[96]{0:T(128)S(1)}, u32[]{:S(2)}) copy-start(f32[96]{0:T(128)S(1)} %add_rsqrt_fusion.2) | copy-start | bytes 1156
  11.9 255.5 %copy-start.1 = (bf16[2,96,1280]{2,1,0:T(8,128)(2,1)S(1)}, bf16[2,96,1280]{2,1,0:T(8,128)(2,1)}, u32[]{:S(2)}) copy-start(bf16[2,96,1280]{2,1,0:T(8,128)(2,1)} %param.6) | copy-start | bytes 1474564
  271.2 18.2 %collective-permute-start = (bf16[96,2560]{1,0:T(8,128)(2,1)S(1)}, bf16[96,2560]{1,0:T(8,128)(2,1)S(1)}, u32[]{:S(2)}, u32[]{:S(2)}) collective-permute-start(bf16[96,2560]{1,0:T(8,128)(2,1)S(1)} %slice.200), channel_id=1, source_target_pairs={{0,1},{1,2},{2,3},{3,4},{4,5},{5,6},{6,7},{7,8},{8,9},{9,10},{10,1... | collective-permute-start | bytes 1474568 | tf_op jit(solution)/shard_map/ppermute | solution.py:16
  276.0 14.6 %copy-start.6 = (bf16[96,3840]{0,1:T(8,128)(2,1)}, bf16[96,3840]{0,1:T(8,128)(2,1)S(1)}, u32[]{:S(2)}) copy-start(bf16[96,3840]{0,1:T(8,128)(2,1)S(1)} %copy.70) | copy-start | bytes 2211844
  290.6 4.9 copy-start.19
  290.6 4.9 copy-start.21
  296.2 2.4 collective-permute-start.1
  298.8 5.6 copy-start.48
  305.2 21.1 %collective-permute-start.2 = (bf16[96,2560]{1,0:T(8,128)(2,1)}, bf16[96,2560]{1,0:T(8,128)(2,1)}, u32[]{:S(2)}, u32[]{:S(2)}) collective-permute-start(bf16[96,2560]{1,0:T(8,128)(2,1)} %slice.206), channel_id=1, source_target_pairs={{0,1},{1,2},{2,3},{3,4},{4,5},{5,6},{6,7},{7,8},{8,9},{9,10},{10,1... | collective-permute-start | bytes 1474568 | tf_op jit(solution)/shard_map/ppermute | solution.py:16
  307.8 20.9 %copy-start.7 = (bf16[96,3840]{0,1:T(8,128)(2,1)}, bf16[96,3840]{0,1:T(8,128)(2,1)S(1)}, u32[]{:S(2)}) copy-start(bf16[96,3840]{0,1:T(8,128)(2,1)S(1)} %copy.73) | copy-start | bytes 2211844
  334.2 2.6 collective-permute-start.3
  343.9 21.1 %collective-permute-start.4 = (bf16[96,2560]{1,0:T(8,128)(2,1)}, bf16[96,2560]{1,0:T(8,128)(2,1)}, u32[]{:S(2)}, u32[]{:S(2)}) collective-permute-start(bf16[96,2560]{1,0:T(8,128)(2,1)} %slice.212), channel_id=1, source_target_pairs={{0,1},{1,2},{2,3},{3,4},{4,5},{5,6},{6,7},{7,8},{8,9},{9,10},{10,1... | collective-permute-start | bytes 1474568 | tf_op jit(solution)/shard_map/ppermute | solution.py:16
  347.3 27.4 %copy-start.52 = (pred[96]{0:T(512)(128)(4,1)}, pred[96]{0:T(512)(128)(4,1)S(1)}, u32[]{:S(2)}) copy-start(pred[96]{0:T(512)(128)(4,1)S(1)} %get-tuple-element.44) | copy-start | bytes 292
  350.4 20.5 %copy-start.40 = (bf16[96,16,80]{0,2,1:T(8,128)(2,1)}, bf16[96,16,80]{0,2,1:T(8,128)(2,1)S(1)}, u32[]{:S(2)}) copy-start(bf16[96,16,80]{0,2,1:T(8,128)(2,1)S(1)} %get-tuple-element.21) | copy-start | bytes 737284
  385.1 6.4 copy-start.35
  387.1 5.5 copy-start.5
  387.1 16.2 %collective-permute-start.5 = (bf16[96,2560]{1,0:T(8,128)(2,1)}, bf16[96,2560]{1,0:T(8,128)(2,1)}, u32[]{:S(2)}, u32[]{:S(2)}) collective-permute-start(bf16[96,2560]{1,0:T(8,128)(2,1)} %pad_maximum_fusion.18), channel_id=1, source_target_pairs={{1,0},{2,1},{3,2},{4,3},{5,4},{6,5},{7,6},{8,7},{9,8},{10,9},{11,1... | collective-permute-start | bytes 1474568 | tf_op jit(solution)/shard_map/ppermute | solution.py:16
  405.4 7.1 copy-start.15
  405.4 7.2 copy-start.17
  405.4 7.2 copy-start.53
  413.4 3.4 collective-permute-start.6
  426.6 10.6 copy-start.3
  429.2 17.5 %collective-permute-start.7 = (bf16[96,2560]{1,0:T(8,128)(2,1)}, bf16[96,2560]{1,0:T(8,128)(2,1)}, u32[]{:S(2)}, u32[]{:S(2)}) collective-permute-start(bf16[96,2560]{1,0:T(8,128)(2,1)} %pad_maximum_fusion.19), channel_id=1, source_target_pairs={{1,0},{2,1},{3,2},{4,3},{5,4},{6,5},{7,6},{8,7},{9,8},{10,9},{11,1... | collective-permute-start | bytes 1474568 | tf_op jit(solution)/shard_map/ppermute | solution.py:16
  448.5 7.1 copy-start.12
  448.5 10.8 copy-start.16
  448.5 10.8 copy-start.55
  455.9 3.4 collective-permute-start.8
  468.4 20.9 %collective-permute-start.9 = (bf16[96,2560]{1,0:T(8,128)(2,1)}, bf16[96,2560]{1,0:T(8,128)(2,1)}, u32[]{:S(2)}, u32[]{:S(2)}) collective-permute-start(bf16[96,2560]{1,0:T(8,128)(2,1)} %pad_maximum_fusion.20), channel_id=1, source_target_pairs={{1,0},{2,1},{3,2},{4,3},{5,4},{6,5},{7,6},{8,7},{9,8},{10,9},{11,1... | collective-permute-start | bytes 1474568 | tf_op jit(solution)/shard_map/ppermute | solution.py:16
  491.1 707.1 %copy-start.27 = (bf16[1,1,96,1280]{3,2,1,0:T(8,128)(2,1)S(1)}, bf16[1,1,96,1280]{3,2,1,0:T(8,128)(2,1)}, u32[]{:S(2)}) copy-start(bf16[1,1,96,1280]{3,2,1,0:T(8,128)(2,1)} %get-tuple-element.32) | copy-start | bytes 737284
  491.1 707.1 %copy-start.29 = (bf16[96,1280]{1,0:T(8,128)(2,1)S(1)}, bf16[96,1280]{1,0:T(8,128)(2,1)}, u32[]{:S(2)}) copy-start(bf16[96,1280]{1,0:T(8,128)(2,1)} %copy-done.28) | copy-start | bytes 737284
  491.1 707.1 %copy-start.32 = (bf16[96,1280]{1,0:T(8,128)(2,1)S(1)}, bf16[96,1280]{1,0:T(8,128)(2,1)}, u32[]{:S(2)}) copy-start(bf16[96,1280]{1,0:T(8,128)(2,1)} %copy-done.31) | copy-start | bytes 737284
  (41 other events, 102.6 us)
Sparse Core Ops, SparseCore 0:
  12.9 244.2 all-gather.1
where the time goes:
time: 1210 us
  blocking collectives  699 us (58%)
  waiting for transfers between devices  304 us (25%)
  matrix products  76.3 us (6%)
  local copies, waits for them, and re-layouts  61.5 us (5%)
  starting transfers between devices  31.1 us (3%)
  other arithmetic  17.6 us (1%)
  between operations  15.7 us (1%)
    unnamed x1, blocking collectives  699 us
    all_gather x1, waiting for transfers between devices, shards(): weight = lax.all_gather(qkv_weight, 'dp', axis=1, tiled=True)[0]  245 us
    ppermute x10, waiting for transfers between devices, passed_along(): return lax.ppermute(x, axis, pairs)  59.2 us
    ppermute x10, starting transfers between devices, passed_along(): return lax.ppermute(x, axis, pairs)  31.1 us
    unnamed x126, local copies, waits for them, and re-layouts  25 us
  transfers between devices with their start and end apart: 11, of which 10 were waited for; matrix products, arithmetic and copies ran while one was open for 3% of the time, Pallas kernels for 0%

commit v1 on v0

v1 whole, which is shorter than its diff:
```python
import functools
import math

import jax
import jax.numpy as jnp
from jax import lax
from jax.experimental import pallas as pl
from jax.experimental.pallas import tpu as pltpu
from jax.sharding import PartitionSpec as P

WIDTH = 1280
HEADS = 16
HEAD_DIM = 80
RUN = 96
PLANE = 16
LAYERS = 16
SIDE = 4
PANEL = 80
TILE = 128
HALF = 640
MESH = pl.DeviceIdType.MESH


def place():
    core = lax.axis_index("phase")
    dp = lax.axis_index("dp")
    z = dp // PLANE
    slot = dp % PLANE
    return core, dp, z, slot, slot // SIDE, slot % SIDE


def greet_plane_and_line(core, z, slot, line):
    barrier = pltpu.get_barrier_semaphore()
    mine = 2 * slot + core

    def plane(j, _):
        @pl.when(j != mine)
        def _():
            pl.semaphore_signal(barrier, inc=1, device_id=(j % 2, PLANE * z + j // 2), device_id_type=MESH)

    lax.fori_loop(0, 2 * PLANE, plane, None)
    if line == "neighbours":
        for step in (1, LAYERS - 1):
            pl.semaphore_signal(
                barrier, inc=1, device_id=(core, PLANE * ((z + step) % LAYERS) + slot), device_id_type=MESH
            )
        pl.semaphore_wait(barrier, 2 * PLANE - 1 + 2)
    else:

        def along(step, _):
            pl.semaphore_signal(
                barrier, inc=1, device_id=(core, PLANE * ((z + step) % LAYERS) + slot), device_id_type=MESH
            )

        lax.fori_loop(1, LAYERS, along, None)
        pl.semaphore_wait(barrier, 2 * PLANE - 1 + LAYERS - 1)


def gather_body(raw, w, sendbuf, stage, psend, pown, precv, zsend, zrecv, rsend, rrecv, ssend, srecv):
    core, dp, z, slot, x, y = place()
    greet_plane_and_line(core, z, slot, "neighbours")
    for c in range(2):
        for n in range(SIDE):
            sendbuf[c, n, :, :TILE] = raw[:, (5 * c + n) * TILE : (5 * c + n + 1) * TILE]
            sendbuf[c, n, :, TILE:] = raw[:, (5 * c + 4) * TILE : (5 * c + 5) * TILE]
    mine = 2 * slot + core

    def piece(j):
        c = j % 2
        i = j // 2
        n = jnp.where(c == 0, i % SIDE, i // SIDE)
        return pltpu.make_async_remote_copy(
            src_ref=sendbuf.at[c, n],
            dst_ref=stage.at[core, slot],
            send_sem=psend.at[j],
            recv_sem=precv.at[core],
            device_id=(c, PLANE * z + i),
            device_id_type=MESH,
        )

    ring_place = jnp.where(core == 0, y, x)
    own_piece = pltpu.make_async_copy(sendbuf.at[core, ring_place], stage.at[core, slot], precv.at[core])
    own_piece.start()

    def send_piece(j, _):
        @pl.when(j != mine)
        def _():
            piece(j).start()

    lax.fori_loop(0, 2 * PLANE, send_piece, None)
    base = 5 * core
    my_tile = base + ring_place
    row = lax.broadcasted_iota(jnp.int32, (3 * PANEL, 16 * PLANE), 0)
    column = lax.broadcasted_iota(jnp.int32, (3 * PANEL, 16 * PLANE), 1)
    within = row % PANEL
    wanted = (within // 5) * 16 + (row // PANEL) * 5 + within % 5
    select = (column == wanted).astype(jnp.float32).astype(jnp.bfloat16)
    rows = pl.ds(pl.multiple_of(PANEL * z, 16), PANEL)
    for s in range(2):
        pltpu.make_async_copy(stage.at[s], stage.at[s], precv.at[s]).wait()
        panel = jnp.dot(
            select, stage[s].reshape(16 * PLANE, 2 * TILE), preferred_element_type=jnp.float32
        ).astype(jnp.bfloat16)
        for t in range(3):
            w[s, t, rows, pl.ds(pl.multiple_of(TILE * my_tile, TILE), TILE)] = panel[
                t * PANEL : (t + 1) * PANEL, :TILE
            ]
            w[s, t, rows, pl.ds(pl.multiple_of(TILE * (base + 4), TILE), TILE)] = panel[
                t * PANEL : (t + 1) * PANEL, TILE:
            ]

    def drain_piece(j, _):
        @pl.when(j != mine)
        def _():
            piece(j).wait_send()

    lax.fori_loop(0, 2 * PLANE, drain_piece, None)

    def region(s, panel, tile, width=TILE):
        return w.at[
            s,
            :,
            pl.ds(pl.multiple_of(PANEL * panel, 16), PANEL),
            pl.ds(pl.multiple_of(TILE * tile, TILE), width),
        ]

    def tile_of(kind):
        return my_tile if kind == 0 else base + 4

    def panel_of(q):
        k = (q + 1) // 2
        sign = jnp.where(q % 2 == 1, -1, 1)
        return (z + sign * k + LAYERS) % LAYERS

    def z_copy(s, kind, panel, upward):
        to = (z + jnp.where(upward == 1, 1, LAYERS - 1)) % LAYERS
        piece_ref = region(s, panel, tile_of(kind))
        return pltpu.make_async_remote_copy(
            src_ref=piece_ref,
            dst_ref=piece_ref,
            send_sem=zsend.at[s, kind, upward, panel],
            recv_sem=zrecv.at[s, kind, panel],
            device_id=(core, PLANE * to + slot),
            device_id_type=MESH,
        )

    def ring_device(step):
        moved = (ring_place + step) % SIDE
        return PLANE * z + jnp.where(core == 0, SIDE * x + moved, SIDE * moved + y)

    def ring_tile(step):
        return base + (ring_place + step) % SIDE

    def ring_copy(s, panel, tile, step, way):
        piece_ref = region(s, panel, tile)
        return pltpu.make_async_remote_copy(
            src_ref=piece_ref,
            dst_ref=piece_ref,
            send_sem=rsend.at[s, panel, way],
            recv_sem=rrecv.at[s, panel, way],
            device_id=(core, ring_device(step)),
            device_id_type=MESH,
        )

    def passed_on(s, panel):
        even = panel % 2 == 0
        tile = jnp.where(even, ring_tile(SIDE - 1), ring_tile(1))
        return ring_copy(s, panel, tile, jnp.where(even, 1, SIDE - 1), 2)

    def sibling_copy(s, panel):
        piece_ref = region(s, panel, base, HALF)
        return pltpu.make_async_remote_copy(
            src_ref=piece_ref,
            dst_ref=piece_ref,
            send_sem=ssend.at[s, panel],
            recv_sem=srecv.at[s, panel],
            device_id=(1 - core, dp),
            device_id_type=MESH,
        )

    def step(i, _):
        @pl.when(i < 32)
        def _():
            s, q = i // 16, i % 16
            panel = panel_of(q)
            upward = q % 2

            @pl.when(q == 0)
            def _():
                for kind in range(2):
                    for way in range(2):
                        z_copy(s, kind, panel, way).start()

            @pl.when(q > 0)
            def _():
                z_copy(s, 0, panel, upward).wait_recv()

                @pl.when(q < 14)
                def _():
                    z_copy(s, 0, panel, upward).start()

                z_copy(s, 1, panel, upward).wait_recv()

                @pl.when((q < 13) | (q == 14))
                def _():
                    z_copy(s, 1, panel, upward).start()

            ring_copy(s, panel, my_tile, 1, 0).start()
            ring_copy(s, panel, my_tile, SIDE - 1, 1).start()

        @pl.when((i >= 1) & (i < 33))
        def _():
            s, q = (i - 1) // 16, (i - 1) % 16
            panel = panel_of(q)
            ring_copy(s, panel, ring_tile(SIDE - 1), 1, 0).wait_recv()
            ring_copy(s, panel, ring_tile(1), 1, 1).wait_recv()
            passed_on(s, panel).start()

        @pl.when(i >= 2)
        def _():
            s, q = (i - 2) // 16, (i - 2) % 16
            panel = panel_of(q)
            ring_copy(s, panel, ring_tile(2), 1, 2).wait_recv()
            sibling_copy(s, panel).start()

    lax.fori_loop(0, 34, step, None)

    def finish(i, _):
        s, q = i // 16, i % 16
        panel = panel_of(q)
        sibling_copy(s, panel).wait()

        for way in range(3):
            ring_copy(s, panel, my_tile, 1, way).wait_send()

        @pl.when(q == 0)
        def _():
            for kind in range(2):
                for way in range(2):
                    z_copy(s, kind, panel, way).wait_send()

        @pl.when((q > 0) & (q < 14))
        def _():
            z_copy(s, 0, panel, q % 2).wait_send()

        @pl.when(((q > 0) & (q < 13)) | (q == 14))
        def _():
            z_copy(s, 1, panel, q % 2).wait_send()

    lax.fori_loop(0, 32, finish, None)


GATHER_SCRATCH = [
    pltpu.VMEM((2, SIDE, 16, 2 * TILE), jnp.bfloat16),
    pltpu.VMEM((2, PLANE, 16, 2 * TILE), jnp.bfloat16),
    pltpu.SemaphoreType.DMA((2 * PLANE,)),
    pltpu.SemaphoreType.DMA,
    pltpu.SemaphoreType.DMA((2,)),
    pltpu.SemaphoreType.DMA((2, 2, 2, LAYERS)),
    pltpu.SemaphoreType.DMA((2, 2, LAYERS)),
    pltpu.SemaphoreType.DMA((2, LAYERS, 3)),
    pltpu.SemaphoreType.DMA((2, LAYERS, 3)),
    pltpu.SemaphoreType.DMA((2, LAYERS)),
    pltpu.SemaphoreType.DMA((2, LAYERS)),
]


def gather_kernel(raw, out, w, outsem, *scratch):
    gather_body(raw, w, *scratch)
    copy = pltpu.make_async_copy(w, out, outsem)
    copy.start()
    copy.wait()


def gathered(shard):
    raw = jnp.transpose(shard.reshape(5, 3, WIDTH), (1, 0, 2)).reshape(15, WIDTH)
    raw = jnp.pad(raw, ((0, 1), (0, 0)))
    return pl.pallas_call(
        gather_kernel,
        out_shape=jax.ShapeDtypeStruct((2, 3, WIDTH, WIDTH), jnp.bfloat16),
        in_specs=[pl.BlockSpec(memory_space=pltpu.VMEM)],
        out_specs=pl.BlockSpec(memory_space=pl.ANY),
        scratch_shapes=[pltpu.VMEM((2, 3, WIDTH, WIDTH), jnp.bfloat16), pltpu.SemaphoreType.DMA]
        + GATHER_SCRATCH,
        compiler_params=pltpu.CompilerParams(
            collective_id=0, has_side_effects=True, vmem_limit_bytes=48 * 2**20
        ),
        name="gather",
    )(raw)


def reduce_kernel(terms, out, part, line, both, plane, lsend, lrecv, psend, precv):
    core, dp, z, slot, x, y = place()
    greet_plane_and_line(core, z, slot, "line")
    for k in range(LAYERS):
        part[k, 0:2, :] = jnp.concatenate(
            [terms[:, PANEL * k : PANEL * (k + 1)], jnp.zeros((2, TILE - PANEL), jnp.float32)], axis=1
        )

    def along(step):
        to = (z + step) % LAYERS
        return pltpu.make_async_remote_copy(
            src_ref=part.at[to],
            dst_ref=line.at[step],
            send_sem=lsend.at[step],
            recv_sem=lrecv.at[step],
            device_id=(core, PLANE * to + slot),
            device_id_type=MESH,
        )

    def start_along(step, _):
        along(step).start()

    lax.fori_loop(1, LAYERS, start_along, None)
    total = part[z, 0:2, :]
    for step in range(1, LAYERS):
        along(step).wait_recv()
        total = total + line[step, 0:2, :]
    both[0] = jnp.broadcast_to(total[0:1], (8, TILE))
    both[1] = jnp.broadcast_to(total[1:2], (8, TILE))
    mine = 2 * slot + core

    def across(j):
        return pltpu.make_async_remote_copy(
            src_ref=both.at[j % 2],
            dst_ref=plane.at[mine],
            send_sem=psend.at[j],
            recv_sem=precv.at[mine],
            device_id=(j % 2, PLANE * z + j // 2),
            device_id_type=MESH,
        )

    def start_across(j, _):
        @pl.when(j != mine)
        def _():
            across(j).start()

    lax.fori_loop(0, 2 * PLANE, start_across, None)
    plane[mine] = both[core]

    def arrive(j, _):
        @pl.when(j != mine)
        def _():
            pltpu.make_async_copy(plane.at[j], plane.at[j], precv.at[j]).wait()

    lax.fori_loop(0, 2 * PLANE, arrive, None)
    out[...] = jnp.sum(plane[...], axis=0)[0:1]

    def drain_along(step, _):
        along(step).wait_send()

    lax.fori_loop(1, LAYERS, drain_along, None)

    def drain_across(j, _):
        @pl.when(j != mine)
        def _():
            across(j).wait_send()

    lax.fori_loop(0, 2 * PLANE, drain_across, None)


def reduced(terms):
    row = pl.pallas_call(
        reduce_kernel,
        out_shape=jax.ShapeDtypeStruct((1, TILE), jnp.float32),
        in_specs=[pl.BlockSpec(memory_space=pltpu.VMEM)],
        out_specs=pl.BlockSpec(memory_space=pltpu.VMEM),
        scratch_shapes=[
            pltpu.VMEM((LAYERS, 8, TILE), jnp.float32),
            pltpu.VMEM((LAYERS, 8, TILE), jnp.float32),
            pltpu.VMEM((2, 8, TILE), jnp.float32),
            pltpu.VMEM((2 * PLANE, 8, TILE), jnp.float32),
            pltpu.SemaphoreType.DMA((LAYERS,)),
            pltpu.SemaphoreType.DMA((LAYERS,)),
            pltpu.SemaphoreType.DMA((2 * PLANE,)),
            pltpu.SemaphoreType.DMA((2 * PLANE,)),
        ],
        compiler_params=pltpu.CompilerParams(collective_id=1, has_side_effects=True),
        name="reduce",
    )(terms)
    slot = lax.axis_index("dp") % PLANE
    return lax.dynamic_slice(row, (0, 5 * slot), (1, 5))


def passed_along(x, axis, by):
    size = lax.axis_size(axis)
    pairs = [(i, i + by) for i in range(size) if 0 <= i + by < size]
    return lax.ppermute(x, axis, pairs)


def heads_of(x):
    return x.reshape(x.shape[0], HEADS, HEAD_DIM).astype(jnp.float32)


def forward(x, w, scaling, allowed):
    widened = x.astype(jnp.float32)
    inverse = lax.rsqrt(jnp.mean(widened * widened, axis=-1, keepdims=True) + 1e-05)
    normed = (widened * inverse * scaling).astype(jnp.bfloat16)
    q, k, v = (jnp.dot(normed, w[t], preferred_element_type=jnp.float32).astype(jnp.bfloat16) for t in range(3))
    remote = passed_along(jnp.concatenate([k, v], axis=1), "dp", 1)
    queries = heads_of(q)
    keys = heads_of(jnp.concatenate([remote[:, :WIDTH], k], axis=0))
    values = heads_of(jnp.concatenate([remote[:, WIDTH:], v], axis=0))
    scores = jnp.einsum("qhd,khd->hqk", queries, keys) / math.sqrt(HEAD_DIM)
    scores = jnp.where(allowed[None], scores, -1e30)
    exponent = jnp.exp(scores - jnp.max(scores, axis=-1, keepdims=True))
    softmax = exponent / jnp.sum(exponent, axis=-1, keepdims=True)
    rounded = softmax.astype(jnp.bfloat16).astype(jnp.float32)
    attended = jnp.einsum("hqk,khd->qhd", rounded, values)
    out = (widened + attended.reshape(RUN, WIDTH)).astype(jnp.bfloat16)
    return out, (widened, inverse, queries, keys, values, softmax, rounded)


def backward(record, w, scaling, upstream):
    widened, inverse, queries, keys, values, softmax, rounded = record
    flowing = upstream.astype(jnp.float32)
    per_head = heads_of(upstream)
    grad_soft = jnp.einsum("qhd,khd->hqk", per_head, values)
    grad_values = jnp.einsum("hqk,qhd->khd", rounded, per_head)
    grad_scores = (
        softmax * (grad_soft - jnp.sum(softmax * grad_soft, axis=-1, keepdims=True)) / math.sqrt(HEAD_DIM)
    )
    grad_q = jnp.einsum("hqk,khd->qhd", grad_scores, keys).reshape(RUN, WIDTH)
    grad_k = jnp.einsum("hqk,qhd->khd", grad_scores, queries).reshape(2 * RUN, WIDTH)
    grad_v = grad_values.reshape(2 * RUN, WIDTH)
    away = jnp.concatenate([grad_k[:RUN], grad_v[:RUN]], axis=1).astype(jnp.bfloat16)
    back = passed_along(away, "dp", -1).astype(jnp.float32)
    grads = (grad_q, grad_k[RUN:] + back[:, :WIDTH], grad_v[RUN:] + back[:, WIDTH:])
    grad_normed = sum(
        lax.dot_general(g.astype(jnp.bfloat16), w[t], (((1,), (1,)), ((), ())), preferred_element_type=jnp.float32)
        for t, g in enumerate(grads)
    )
    gain = jnp.sum(grad_normed * widened * inverse, axis=0)
    scaled = grad_normed * scaling
    grad_in = inverse * (scaled - widened * inverse * inverse * jnp.mean(scaled * widened, axis=-1, keepdims=True))
    return (flowing + grad_in).astype(jnp.bfloat16), gain


def shards(tokens, segment_ids, loss_mask, qkv_weight, gains, cotangent):
    core = lax.axis_index("phase")
    dp = lax.axis_index("dp")
    w = gathered(qkv_weight[0])
    other = lax.ppermute(gains, "phase", [(0, 1), (1, 0)])
    scale = jnp.where(core == 0, jnp.concatenate([gains, other]), jnp.concatenate([other, gains]))
    x = jnp.where(core == 0, tokens[0], tokens[1])
    seg = jnp.where(core == 0, segment_ids[0], segment_ids[1])
    seg_own = lax.dynamic_slice_in_dim(seg, dp * RUN, RUN)
    seg_prev = lax.dynamic_slice_in_dim(seg, jnp.maximum(dp - 1, 0) * RUN, RUN)
    position = jnp.arange(RUN)
    own_ok = (seg_own[:, None] == seg_own[None, :]) & (position[None, :] <= position[:, None])
    prev_ok = (seg_own[:, None] == seg_prev[None, :]) & (dp > 0)
    allowed = jnp.concatenate([prev_ok, own_ok], axis=1)
    middle, first = forward(x, w[0], scale[0], allowed)
    final, second = forward(middle, w[1], scale[1], allowed)
    cot = jnp.where(core == 0, cotangent[0], cotangent[1])
    mask = jnp.where(core == 0, loss_mask[0], loss_mask[1])
    upstream = jnp.where(mask[:, None] == 1, cot, jnp.zeros((), jnp.bfloat16))
    middle_grad, gain_second = backward(second, w[1], scale[1], upstream)
    grad, gain_first = backward(first, w[0], scale[0], middle_grad)
    handed = jnp.where(core == 0, final, grad)
    kept = jnp.where(core == 0, grad, final)
    got = lax.ppermute(handed, "phase", [(0, 1), (1, 0)])
    boundary = jnp.where(core == 0, jnp.stack([kept, got]), jnp.stack([got, kept]))[None]
    return boundary, reduced(jnp.stack([gain_first, gain_second]))


def solution(mesh):
    in_specs = (
        P(None, "dp", None),
        P(),
        P(None, "dp"),
        P("phase", "dp", None),
        P("phase", None),
        P(None, "dp", None),
    )
    out_specs = (P("phase", None, "dp", None), P("phase", "dp"))
    return jax.shard_map(shards, mesh=mesh, in_specs=in_specs, out_specs=out_specs, check_vma=False)
```

time: 1210 us -> 281 us (0.23)
  the two profiles are of different devices: /device:TPU:128 before, /device:TPU:1 now
where the time goes in v1:
time: 281 us; the launch traced here: 280 us
  Pallas kernels  153 us (54%)
  matrix products  57.3 us (20%)
  starting transfers between devices  24.9 us (9%)
  waiting for transfers between devices  20.1 us (7%)
  local copies, waits for them, and re-layouts  12.3 us (4%)
  other arithmetic  10.1 us (4%)
    pallas_call x1, Pallas kernels, gathered(): pl.pallas_call(gather_kernel, out_shape=jax.ShapeDtypeStruct((2, 3, WIDTH...  115 us
    pallas_call x1, Pallas kernels, reduced(): pl.pallas_call(reduce_kernel, out_shape=jax.ShapeDtypeStruct((1, TILE), j...  38.7 us
    ppermute x4, waiting for transfers between devices, passed_along(): return lax.ppermute(x, axis, pairs)  20.1 us
    dot_general x6, matrix products, backward(): lax.dot_general(g.astype(jnp.bfloat16), w[t], (((1,), (1,)), ((), ())), p...  19 us
    dot_general x6, matrix products, forward(): jnp.dot(normed, w[t], preferred_element_type=jnp.float32)  15.8 us
    ppermute x4, starting transfers between devices, passed_along(): return lax.ppermute(x, axis, pairs)  10.5 us
    ppermute x1, starting transfers between devices, shards(): other = lax.ppermute(gains, 'phase', [(0, 1), (1, 0)])  8.92 us
    dot_general x2, matrix products, backward(): grad_soft = jnp.einsum('qhd,khd->hqk', per_head, values)  5.7 us
  transfers between devices with their start and end apart: 6, of which 4 were waited for; matrix products, arithmetic and copies ran while one was open for 10% of the time, Pallas kernels for 55%

profile of v1, /device:TPU:1, one launch (start us, length us, event | category | flops | bytes accessed | tf_op | source)
XLA Modules:
  0.0 279.6 jit_solution(16493458011009224479)
XLA Ops:
  0.6 8.9 %collective-permute-start = (f32[1,1280]{1,0:T(1,128)}, f32[1,1280]{1,0:T(1,128)S(1)}, u32[]{:S(2)}, u32[]{:S(2)}) collective-permute-start(f32[1,1280]{1,0:T(1,128)} %param.10), channel_id=1, source_target_pairs={{0,256},{256,0},{1,257},{257,1},{2,258},{258,2},{3,259},{259,3},{4... | collective-permute-start | bytes 15368 | tf_op jit(solution)/shard_map/ppermute | solution.py:443
  13.3 114.7 %gather.1 = bf16[2,3,1280,1280]{3,2,1,0:T(8,128)(2,1)} custom-call(bf16[16,1280]{1,0:T(8,128)(2,1)S(1)} %pad.4.raw), custom_call_target="tpu_custom_call" | custom-call | tf_op jit(solution)/shard_map/gather/pallas_call | solution.py:278
  128.1 2.6 fusion.53
  130.7 2.6 fusion.50
  133.4 3.2 %collective-permute-start.1 = (bf16[96,2560]{1,0:T(8,128)(2,1)S(1)}, bf16[96,2560]{1,0:T(8,128)(2,1)S(1)}, u32[]{:S(2)}, u32[]{:S(2)}) collective-permute-start(bf16[96,2560]{1,0:T(8,128)(2,1)S(1)} %pad_maximum_fusion), channel_id=1, source_target_pairs={{0,1},{1,2},{2,3},{3,4},{4,5},{5,6},{6,7},{7,8},{8,9},{9,10},{10,1... | collective-permute-start | bytes 1474568 | tf_op jit(solution)/shard_map/ppermute | solution.py:388
  138.0 2.6 fusion.56
  140.9 6.0 %collective-permute-done.1 = bf16[96,2560]{1,0:T(8,128)(2,1)S(1)} collective-permute-done((bf16[96,2560]{1,0:T(8,128)(2,1)S(1)}, bf16[96,2560]{1,0:T(8,128)(2,1)S(1)}, u32[]{:S(2)}, u32[]{:S(2)}) %collective-permute-start.1) | collective-permute-done | bytes 491552 | tf_op jit(solution)/shard_map/ppermute | solution.py:388
  147.5 1.8 fusion.140
  149.3 1.9 fusion.72
  151.5 2.6 fusion.62
  154.1 2.6 fusion.59
  156.8 4.3 %collective-permute-start.2 = (bf16[96,2560]{1,0:T(8,128)(2,1)S(1)}, bf16[96,2560]{1,0:T(8,128)(2,1)S(1)}, u32[]{:S(2)}, u32[]{:S(2)}) collective-permute-start(bf16[96,2560]{1,0:T(8,128)(2,1)S(1)} %pad_maximum_fusion.3), channel_id=1, source_target_pairs={{0,1},{1,2},{2,3},{3,4},{4,5},{5,6},{6,7},{7,8},{8,9},{9,10},{10,1... | collective-permute-start | bytes 1474568 | tf_op jit(solution)/shard_map/ppermute | solution.py:388
  161.2 2.6 fusion.65
  164.9 5.3 %collective-permute-done.2 = bf16[96,2560]{1,0:T(8,128)(2,1)S(1)} collective-permute-done((bf16[96,2560]{1,0:T(8,128)(2,1)S(1)}, bf16[96,2560]{1,0:T(8,128)(2,1)S(1)}, u32[]{:S(2)}, u32[]{:S(2)}) %collective-permute-start.2) | collective-permute-done | bytes 491552 | tf_op jit(solution)/shard_map/ppermute | solution.py:388
  171.3 1.9 fusion.141
  173.2 2.3 multiply_reduce_fusion.1
  175.5 1.5 convolution_convert_fusion.1
  181.4 2.0 fusion.103
  184.2 3.2 %fusion.2 = f32[96,1280]{1,0:T(8,128)S(1)} fusion(bf16[96,1280]{0,1:T(8,128)(2,1)} %bitcast.198, bf16[2,3,1280,1280]{3,2,1,0:T(8,128)(2,1)} %gather.1), kind=kOutput, calls=%fused_computation.2 | convolution fusion | flops 314572800 | bytes 4096000 | tf_op jit(solution)/shard_map/dot_general | solution.py:430
  187.4 6.7 %collective-permute-done.3 = bf16[96,2560]{1,0:T(8,128)(2,1)} collective-permute-done((bf16[96,2560]{1,0:T(8,128)(2,1)}, bf16[96,2560]{1,0:T(8,128)(2,1)}, u32[]{:S(2)}, u32[]{:S(2)}) %collective-permute-start.3) | collective-permute-done | bytes 491552 | tf_op jit(solution)/shard_map/ppermute | solution.py:388
  195.1 3.1 %fusion.6 = f32[96,1280]{1,0:T(8,128)S(1)} fusion(bf16[2,3,1280,1280]{3,2,1,0:T(8,128)(2,1)} %gather.1, f32[96,1280]{1,0:T(8,128)S(1)} %copy.51, f32[96,2560]{1,0:T(8,128)S(1)} %convert_element_type.166), kind=kOutput, calls=%fused_computation.6 | convolution fusion | flops 314818560 | bytes 4751360 | tf_op jit(solution)/shard_map/dot_general | solution.py:430
  198.2 3.3 %fusion.85 = (f32[1280]{0:T(1024)S(1)}, f32[96]{0:T(128)S(1)}, bf16[96,1280]{1,0:T(8,128)(2,1)S(1)}, f32[96,1280]{1,0:T(8,128)S(1)}) fusion(f32[96]{0:T(128)S(1)} %add_rsqrt_fusion, f32[1280]{0:T(1024)S(1)} %get-tuple-element.6, f32[96,1280]{1,0:T(8,128)S(1)} %copy.52, bf16[1,96,1280]{2,1,0:T(8,128)(2,1)S(1)} %get-tuple-element.14, ...), kind=kOutput, calls=%fused_computation.90 | convolution fusion | flops 316291744 | bytes 6731648 | tf_op jit(solution)/shard_map/dot_general | solution.py:430
  202.6 3.4 %multiply_reduce_fusion = (f32[16,96]{1,0:T(8,128)S(1)}, f32[16,96,192]{2,1,0:T(8,128)}) fusion(f32[16,96,192]{2,1,0:T(8,128)} %get-tuple-element.24, f32[16,96]{1,0:T(8,128)S(1)} %copy-done.22, bf16[96,16,80]{0,2,1:T(8,128)(2,1)S(1)} %bitcast.194, bf16[192,16,80]{0,2,1:T(8,128)(2,1)S(1)} %bitcast.181), kind=kOutput, calls=%fused_computation.51 | convolution fusion | flops 48069120 | bytes 3108864 | tf_op jit(solution)/shard_map/qhd,khd->hqk/dot_general | solution.py:418
  207.8 2.6 convolution_bitcast_fusion
  212.5 1.6 collective-permute-start.4
  214.1 3.3 %convolution_convert_fusion = bf16[16,80,96]{2,1,0:T(8,128)(2,1)} fusion(bf16[192,16,80]{0,2,1:T(8,128)(2,1)S(1)} %bitcast.179, f32[16,96,192]{2,1,0:T(8,128)} %get-tuple-element.32, f32[16,96]{1,0:T(8,128)S(1)} %get-tuple-element.31, f32[16,96,192]{2,1,0:T(8,128)} %get-tuple-element.24, f32[16,96]{1,0:T(8,128)S(1)} %copy-done.22), kind=kOutput, calls=%fused_computation.62 | convolution fusion | flops 48488448 | bytes 3108864 | tf_op jit(solution)/shard_map/hqk,khd->qhd/dot_general | solution.py:423
  219.5 3.2 %fusion.14 = f32[96,1280]{1,0:T(8,128)S(1)} fusion(bf16[96,1280]{0,1:T(8,128)(2,1)} %bitcast.199, bf16[2,3,1280,1280]{3,2,1,0:T(8,128)(2,1)} %gather.1), kind=kOutput, calls=%fused_computation.14 | convolution fusion | flops 314572800 | bytes 4096000 | tf_op jit(solution)/shard_map/dot_general | solution.py:430
  222.7 2.1 collective-permute-done.4
  225.9 3.1 %fusion.18 = f32[96,1280]{1,0:T(8,128)S(1)} fusion(bf16[2,3,1280,1280]{3,2,1,0:T(8,128)(2,1)} %gather.1, f32[96,1280]{1,0:T(8,128)S(1)} %copy.57, f32[96,2560]{1,0:T(8,128)S(1)} %convert_element_type.176), kind=kOutput, calls=%fused_computation.18 | convolution fusion | flops 314818560 | bytes 4751360 | tf_op jit(solution)/shard_map/dot_general | solution.py:430
  229.0 3.2 %fusion.102 = (f32[1280]{0:T(1024)S(1)}, f32[96]{0:T(128)S(1)}, f32[96,1280]{1,0:T(8,128)S(1)}) fusion(bf16[1,96,1280]{2,1,0:T(8,128)(2,1)S(1)} %get-tuple-element.14, f32[96]{0:T(128)S(1)} %add_rsqrt_fusion.1, f32[1280]{0:T(1024)S(1)} %get-tuple-element.7, f32[96,1280]{1,0:T(8,128)S(1)} %fusion.18, f32[96,1280]{1,0:T(8,128)S(1)} %fusion.14, ...), kind=kOutput, calls=%fused_computation.126 | convolution fusion | flops 315923104 | bytes 5994368 | tf_op jit(solution)/shard_map/dot_general | solution.py:430
  232.6 5.5 %collective-permute-start.5 = (bf16[96,1280]{1,0:T(8,128)(2,1)S(1)}, bf16[96,1280]{1,0:T(8,128)(2,1)S(1)}, u32[]{:S(2)}, u32[]{:S(2)}) collective-permute-start(bf16[96,1280]{1,0:T(8,128)(2,1)S(1)} %broadcast_select_fusion.3), channel_id=1, source_target_pairs={{0,256},{256,0},{1,257},{257,1},{2,258},{258,2},{3,259},{259,3},{4... | collective-permute-start | bytes 737288 | tf_op jit(solution)/shard_map/ppermute | solution.py:462
  238.8 38.7 %reduce.7 = f32[1,128]{1,0:T(1,128)} custom-call(f32[2,1280]{1,0:T(2,128)} %pad_maximum_fusion.8.terms), custom_call_target="tpu_custom_call" | custom-call | tf_op jit(solution)/shard_map/reduce/pallas_call | solution.py:363
  (115 shorter events, 25.5 us)
Async XLA Ops:
  0.6 12.6 %copy-start.14 = (bf16[1,5,3840]{2,1,0:T(8,128)(2,1)S(1)}, bf16[1,5,3840]{2,1,0:T(8,128)(2,1)}, u32[]{:S(2)}) copy-start(bf16[1,5,3840]{2,1,0:T(8,128)(2,1)} %param.9) | copy-start | bytes 115204
  0.6 127.4 %collective-permute-start = (f32[1,1280]{1,0:T(1,128)}, f32[1,1280]{1,0:T(1,128)S(1)}, u32[]{:S(2)}, u32[]{:S(2)}) collective-permute-start(f32[1,1280]{1,0:T(1,128)} %param.10), channel_id=1, source_target_pairs={{0,256},{256,0},{1,257},{257,1},{2,258},{258,2},{3,259},{259,3},{4... | collective-permute-start | bytes 15368 | tf_op jit(solution)/shard_map/ppermute | solution.py:443
  13.3 114.8 %copy-start.15 = (f32[1,1280]{1,0:T(1,128)S(1)}, f32[1,1280]{1,0:T(1,128)}, u32[]{:S(2)}) copy-start(f32[1,1280]{1,0:T(1,128)} %param.10) | copy-start | bytes 15364
  133.4 13.5 %collective-permute-start.1 = (bf16[96,2560]{1,0:T(8,128)(2,1)S(1)}, bf16[96,2560]{1,0:T(8,128)(2,1)S(1)}, u32[]{:S(2)}, u32[]{:S(2)}) collective-permute-start(bf16[96,2560]{1,0:T(8,128)(2,1)S(1)} %pad_maximum_fusion), channel_id=1, source_target_pairs={{0,1},{1,2},{2,3},{3,4},{4,5},{5,6},{6,7},{7,8},{8,9},{9,10},{10,1... | collective-permute-start | bytes 1474568 | tf_op jit(solution)/shard_map/ppermute | solution.py:388
  140.9 6.6 %copy-start.10 = (bf16[96,1280]{0,1:T(8,128)(2,1)}, bf16[96,1280]{0,1:T(8,128)(2,1)S(1)}, u32[]{:S(2)}) copy-start(bf16[96,1280]{0,1:T(8,128)(2,1)S(1)} %copy.42) | copy-start | bytes 737284
  147.2 2.1 copy-start.7
  147.5 3.7 %copy-start.5 = (bf16[192,1280]{0,1:T(8,128)(2,1)}, bf16[192,1280]{0,1:T(8,128)(2,1)S(1)}, u32[]{:S(2)}) copy-start(bf16[192,1280]{0,1:T(8,128)(2,1)S(1)} %copy.43) | copy-start | bytes 1474564
  149.3 1.9 copy-start.21
  154.1 7.0 %copy-start.18 = (s32[2,96]{1,0:T(2,128)S(1)}, s32[2,96]{1,0:T(2,128)}, u32[]{:S(2)}) copy-start(s32[2,96]{1,0:T(2,128)} %param.8) | copy-start | bytes 2308
  156.8 13.5 %collective-permute-start.2 = (bf16[96,2560]{1,0:T(8,128)(2,1)S(1)}, bf16[96,2560]{1,0:T(8,128)(2,1)S(1)}, u32[]{:S(2)}, u32[]{:S(2)}) collective-permute-start(bf16[96,2560]{1,0:T(8,128)(2,1)S(1)} %pad_maximum_fusion.3), channel_id=1, source_target_pairs={{0,1},{1,2},{2,3},{3,4},{4,5},{5,6},{6,7},{7,8},{8,9},{9,10},{10,1... | collective-permute-start | bytes 1474568 | tf_op jit(solution)/shard_map/ppermute | solution.py:388
  161.1 16.8 %copy-start.16 = (pred[96]{0:T(512)(128)(4,1)}, pred[96]{0:T(512)(128)(4,1)S(1)}, u32[]{:S(2)}) copy-start(pred[96]{0:T(512)(128)(4,1)S(1)} %compare_bitcast_fusion) | copy-start | bytes 292
  170.3 1.0 copy-start.13
  170.9 4.6 %copy-start.9 = (bf16[192,1280]{0,1:T(8,128)(2,1)}, bf16[192,1280]{0,1:T(8,128)(2,1)S(1)}, u32[]{:S(2)}) copy-start(bf16[192,1280]{0,1:T(8,128)(2,1)S(1)} %copy.47) | copy-start | bytes 1474564
  170.9 2.3 copy-start.12
  173.2 2.3 copy-start.20
  180.2 13.9 %collective-permute-start.3 = (bf16[96,2560]{1,0:T(8,128)(2,1)}, bf16[96,2560]{1,0:T(8,128)(2,1)}, u32[]{:S(2)}, u32[]{:S(2)}) collective-permute-start(bf16[96,2560]{1,0:T(8,128)(2,1)} %pad_maximum_fusion.6), channel_id=1, source_target_pairs={{1,0},{2,1},{3,2},{4,3},{5,4},{6,5},{7,6},{8,7},{9,8},{10,9},{11,1... | collective-permute-start | bytes 1474568 | tf_op jit(solution)/shard_map/ppermute | solution.py:388
  198.2 3.4 %copy-start = (bf16[2,96,1280]{2,1,0:T(8,128)(2,1)S(1)}, bf16[2,96,1280]{2,1,0:T(8,128)(2,1)}, u32[]{:S(2)}) copy-start(bf16[2,96,1280]{2,1,0:T(8,128)(2,1)} %param.11) | copy-start | bytes 1474564
  198.2 3.4 %copy-start.17 = (pred[96]{0:T(512)(128)(4,1)S(1)}, pred[96]{0:T(512)(128)(4,1)}, u32[]{:S(2)}) copy-start(pred[96]{0:T(512)(128)(4,1)} %copy-done.16) | copy-start | bytes 292
  201.5 1.1 copy-start.8
  201.6 1.1 copy-start.22
  202.6 3.4 %copy-start.19 = (f32[16,96,192]{2,1,0:T(8,128)S(1)}, f32[16,96,192]{2,1,0:T(8,128)}, u32[]{:S(2)}) copy-start(f32[16,96,192]{2,1,0:T(8,128)} %get-tuple-element.24) | copy-start | bytes 3538948
  206.0 1.8 copy-start.11
  206.5 1.1 copy-start.1
  210.4 1.1 copy-start.3
  210.4 3.8 %copy-start.6 = (bf16[192,1280]{0,1:T(8,128)(2,1)S(1)}, bf16[192,1280]{0,1:T(8,128)(2,1)}, u32[]{:S(2)}) copy-start(bf16[192,1280]{0,1:T(8,128)(2,1)} %copy-done.5) | copy-start | bytes 1474564
  212.5 5.0 %copy-start.2 = (f32[192,16,80]{0,2,1:T(8,128)S(1)}, f32[192,16,80]{0,2,1:T(8,128)}, u32[]{:S(2)}) copy-start(f32[192,16,80]{0,2,1:T(8,128)} %copy-done.1) | copy-start | bytes 2949124
  212.5 12.3 %collective-permute-start.4 = (bf16[96,2560]{1,0:T(8,128)(2,1)}, bf16[96,2560]{1,0:T(8,128)(2,1)}, u32[]{:S(2)}, u32[]{:S(2)}) collective-permute-start(bf16[96,2560]{1,0:T(8,128)(2,1)} %pad_maximum_fusion.7), channel_id=1, source_target_pairs={{1,0},{2,1},{3,2},{4,3},{5,4},{6,5},{7,6},{8,7},{9,8},{10,9},{11,1... | collective-permute-start | bytes 1474568 | tf_op jit(solution)/shard_map/ppermute | solution.py:388
  217.5 1.3 copy-start.4
  232.6 46.2 %collective-permute-start.5 = (bf16[96,1280]{1,0:T(8,128)(2,1)S(1)}, bf16[96,1280]{1,0:T(8,128)(2,1)S(1)}, u32[]{:S(2)}, u32[]{:S(2)}) collective-permute-start(bf16[96,1280]{1,0:T(8,128)(2,1)S(1)} %broadcast_select_fusion.3), channel_id=1, source_target_pairs={{0,256},{256,0},{1,257},{257,1},{2,258},{258,2},{3,259},{259,3},{4... | collective-permute-start | bytes 737288 | tf_op jit(solution)/shard_map/ppermute | solution.py:462

commit v2 on v1

v2 whole, which is shorter than its diff:
```python
import functools
import math

import jax
import jax.numpy as jnp
from jax import lax
from jax.experimental import pallas as pl
from jax.experimental.pallas import tpu as pltpu
from jax.sharding import PartitionSpec as P

WIDTH = 1280
HEADS = 16
HEAD_DIM = 80
RUN = 96
PLANE = 16
LAYERS = 16
SIDE = 4
PANEL = 80
TILE = 128
HALF = 640
RING_LAG = 4
CHIP_LAG = 8
DEVICES = 256
NEVER = -1e30
MESH = pl.DeviceIdType.MESH


def place():
    core = lax.axis_index("phase")
    dp = lax.axis_index("dp")
    z = dp // PLANE
    slot = dp % PLANE
    return core, dp, z, slot, slot // SIDE, slot % SIDE


def greet(core, dp, z, slot):
    barrier = pltpu.get_barrier_semaphore()
    mine = 2 * slot + core

    def plane(j, _):
        @pl.when(j != mine)
        def _():
            pl.semaphore_signal(barrier, inc=1, device_id=(j % 2, PLANE * z + j // 2), device_id_type=MESH)

    lax.fori_loop(0, 2 * PLANE, plane, None)

    def along(step, _):
        pl.semaphore_signal(
            barrier, inc=1, device_id=(core, PLANE * ((z + step) % LAYERS) + slot), device_id_type=MESH
        )

    lax.fori_loop(1, LAYERS, along, None)
    for step in (1, DEVICES - 1):
        pl.semaphore_signal(barrier, inc=1, device_id=(core, (dp + step) % DEVICES), device_id_type=MESH)
    pl.semaphore_wait(barrier, 2 * PLANE - 1 + LAYERS - 1 + 2)


def gather_body(raw, w, sendbuf, stage, psend, pown, precv, zsend, zrecv, rsend, rrecv, ssend, srecv):
    core, dp, z, slot, x, y = place()
    for c in range(2):
        for n in range(SIDE):
            sendbuf[c, n, :, :TILE] = raw[:, (5 * c + n) * TILE : (5 * c + n + 1) * TILE]
            sendbuf[c, n, :, TILE:] = raw[:, (5 * c + 4) * TILE : (5 * c + 5) * TILE]
    mine = 2 * slot + core

    def piece(j):
        c = j % 2
        i = j // 2
        n = jnp.where(c == 0, i % SIDE, i // SIDE)
        return pltpu.make_async_remote_copy(
            src_ref=sendbuf.at[c, n],
            dst_ref=stage.at[core, slot],
            send_sem=psend.at[j],
            recv_sem=precv.at[core],
            device_id=(c, PLANE * z + i),
            device_id_type=MESH,
        )

    ring_place = jnp.where(core == 0, y, x)
    own_piece = pltpu.make_async_copy(sendbuf.at[core, ring_place], stage.at[core, slot], precv.at[core])
    own_piece.start()

    def send_piece(j, _):
        @pl.when(j != mine)
        def _():
            piece(j).start()

    lax.fori_loop(0, 2 * PLANE, send_piece, None)
    base = 5 * core
    my_tile = base + ring_place
    row = lax.broadcasted_iota(jnp.int32, (3 * PANEL, 16 * PLANE), 0)
    column = lax.broadcasted_iota(jnp.int32, (3 * PANEL, 16 * PLANE), 1)
    within = row % PANEL
    wanted = (within // 5) * 16 + (row // PANEL) * 5 + within % 5
    select = (column == wanted).astype(jnp.float32).astype(jnp.bfloat16)
    rows = pl.ds(pl.multiple_of(PANEL * z, 16), PANEL)
    for s in range(2):
        pltpu.make_async_copy(stage.at[s], stage.at[s], precv.at[s]).wait()
        panel = jnp.dot(
            select, stage[s].reshape(16 * PLANE, 2 * TILE), preferred_element_type=jnp.float32
        ).astype(jnp.bfloat16)
        for t in range(3):
            w[s, t, rows, pl.ds(pl.multiple_of(TILE * my_tile, TILE), TILE)] = panel[
                t * PANEL : (t + 1) * PANEL, :TILE
            ]
            w[s, t, rows, pl.ds(pl.multiple_of(TILE * (base + 4), TILE), TILE)] = panel[
                t * PANEL : (t + 1) * PANEL, TILE:
            ]

    def drain_piece(j, _):
        @pl.when(j != mine)
        def _():
            piece(j).wait_send()

    lax.fori_loop(0, 2 * PLANE, drain_piece, None)

    def region(s, panel, tile, width=TILE):
        return w.at[
            s,
            :,
            pl.ds(pl.multiple_of(PANEL * panel, 16), PANEL),
            pl.ds(pl.multiple_of(TILE * tile, TILE), width),
        ]

    def tile_of(kind):
        return my_tile if kind == 0 else base + 4

    def panel_of(q):
        k = (q + 1) // 2
        sign = jnp.where(q % 2 == 1, -1, 1)
        return (z + sign * k + LAYERS) % LAYERS

    def z_copy(s, kind, panel, upward):
        to = (z + jnp.where(upward == 1, 1, LAYERS - 1)) % LAYERS
        piece_ref = region(s, panel, tile_of(kind))
        return pltpu.make_async_remote_copy(
            src_ref=piece_ref,
            dst_ref=piece_ref,
            send_sem=zsend.at[s, kind, upward, panel],
            recv_sem=zrecv.at[s, kind, panel],
            device_id=(core, PLANE * to + slot),
            device_id_type=MESH,
        )

    def ring_device(step):
        moved = (ring_place + step) % SIDE
        return PLANE * z + jnp.where(core == 0, SIDE * x + moved, SIDE * moved + y)

    def ring_tile(step):
        return base + (ring_place + step) % SIDE

    def ring_copy(s, panel, tile, step, way):
        piece_ref = region(s, panel, tile)
        return pltpu.make_async_remote_copy(
            src_ref=piece_ref,
            dst_ref=piece_ref,
            send_sem=rsend.at[s, panel, way],
            recv_sem=rrecv.at[s, panel, way],
            device_id=(core, ring_device(step)),
            device_id_type=MESH,
        )

    def passed_on(s, panel):
        even = panel % 2 == 0
        tile = jnp.where(even, ring_tile(SIDE - 1), ring_tile(1))
        return ring_copy(s, panel, tile, jnp.where(even, 1, SIDE - 1), 2)

    def sibling_copy(s, panel):
        piece_ref = region(s, panel, base, HALF)
        return pltpu.make_async_remote_copy(
            src_ref=piece_ref,
            dst_ref=piece_ref,
            send_sem=ssend.at[s, panel],
            recv_sem=srecv.at[s, panel],
            device_id=(1 - core, dp),
            device_id_type=MESH,
        )

    def step(i, _):
        @pl.when(i < 32)
        def _():
            s, q = i % 2, i // 2
            panel = panel_of(q)
            upward = q % 2

            @pl.when(q == 0)
            def _():
                for kind in range(2):
                    for way in range(2):
                        z_copy(s, kind, panel, way).start()

            @pl.when(q > 0)
            def _():
                z_copy(s, 0, panel, upward).wait_recv()

                @pl.when(q < 14)
                def _():
                    z_copy(s, 0, panel, upward).start()

                z_copy(s, 1, panel, upward).wait_recv()

                @pl.when((q < 13) | (q == 14))
                def _():
                    z_copy(s, 1, panel, upward).start()

            ring_copy(s, panel, my_tile, 1, 0).start()
            ring_copy(s, panel, my_tile, SIDE - 1, 1).start()

        @pl.when((i >= RING_LAG) & (i < 32 + RING_LAG))
        def _():
            s, q = (i - RING_LAG) % 2, (i - RING_LAG) // 2
            panel = panel_of(q)
            ring_copy(s, panel, ring_tile(SIDE - 1), 1, 0).wait_recv()
            ring_copy(s, panel, ring_tile(1), 1, 1).wait_recv()
            passed_on(s, panel).start()

        @pl.when(i >= CHIP_LAG)
        def _():
            s, q = (i - CHIP_LAG) % 2, (i - CHIP_LAG) // 2
            panel = panel_of(q)
            ring_copy(s, panel, ring_tile(2), 1, 2).wait_recv()
            sibling_copy(s, panel).start()

    lax.fori_loop(0, 32 + CHIP_LAG, step, None)

    def arrive(i, _):
        sibling_copy(i // 16, i % 16).wait_recv()

    lax.fori_loop(0, 32, arrive, None)

    def finish(i, _):
        s, q = i // 16, i % 16
        panel = panel_of(q)
        sibling_copy(s, panel).wait_send()

        for way in range(3):
            ring_copy(s, panel, my_tile, 1, way).wait_send()

        @pl.when(q == 0)
        def _():
            for kind in range(2):
                for way in range(2):
                    z_copy(s, kind, panel, way).wait_send()

        @pl.when((q > 0) & (q < 14))
        def _():
            z_copy(s, 0, panel, q % 2).wait_send()

        @pl.when(((q > 0) & (q < 13)) | (q == 14))
        def _():
            z_copy(s, 1, panel, q % 2).wait_send()

    return lambda: lax.fori_loop(0, 32, finish, None)


GATHER_SCRATCH = [
    pltpu.VMEM((2, SIDE, 16, 2 * TILE), jnp.bfloat16),
    pltpu.VMEM((2, PLANE, 16, 2 * TILE), jnp.bfloat16),
    pltpu.SemaphoreType.DMA((2 * PLANE,)),
    pltpu.SemaphoreType.DMA,
    pltpu.SemaphoreType.DMA((2,)),
    pltpu.SemaphoreType.DMA((2, 2, 2, LAYERS)),
    pltpu.SemaphoreType.DMA((2, 2, LAYERS)),
    pltpu.SemaphoreType.DMA((2, LAYERS, 3)),
    pltpu.SemaphoreType.DMA((2, LAYERS, 3)),
    pltpu.SemaphoreType.DMA((2, LAYERS)),
    pltpu.SemaphoreType.DMA((2, LAYERS)),
]


def reduce_body(terms, out, part, line, both, plane, lsend, lrecv, psend, precv):
    core, dp, z, slot, x, y = place()
    for k in range(LAYERS):
        part[k, 0:2, :] = jnp.concatenate(
            [terms[0:2, PANEL * k : PANEL * (k + 1)], jnp.zeros((2, TILE - PANEL), jnp.float32)], axis=1
        )

    def along(step):
        to = (z + step) % LAYERS
        return pltpu.make_async_remote_copy(
            src_ref=part.at[to],
            dst_ref=line.at[step],
            send_sem=lsend.at[step],
            recv_sem=lrecv.at[step],
            device_id=(core, PLANE * to + slot),
            device_id_type=MESH,
        )

    def start_along(step, _):
        along(step).start()

    lax.fori_loop(1, LAYERS, start_along, None)
    total = part[z, 0:2, :]
    for step in range(1, LAYERS):
        along(step).wait_recv()
        total = total + line[step, 0:2, :]
    both[0] = jnp.broadcast_to(total[0:1], (8, TILE))
    both[1] = jnp.broadcast_to(total[1:2], (8, TILE))
    mine = 2 * slot + core

    def across(j):
        return pltpu.make_async_remote_copy(
            src_ref=both.at[j % 2],
            dst_ref=plane.at[mine],
            send_sem=psend.at[j],
            recv_sem=precv.at[mine],
            device_id=(j % 2, PLANE * z + j // 2),
            device_id_type=MESH,
        )

    def start_across(j, _):
        @pl.when(j != mine)
        def _():
            across(j).start()

    lax.fori_loop(0, 2 * PLANE, start_across, None)
    plane[mine] = both[core]

    def arrive(j, _):
        @pl.when(j != mine)
        def _():
            pltpu.make_async_copy(plane.at[j], plane.at[j], precv.at[j]).wait()

    lax.fori_loop(0, 2 * PLANE, arrive, None)
    out[...] = jnp.sum(plane[...], axis=0)[0:1]

    def drain_along(step, _):
        along(step).wait_send()

    lax.fori_loop(1, LAYERS, drain_along, None)

    def drain_across(j, _):
        @pl.when(j != mine)
        def _():
            across(j).wait_send()

    lax.fori_loop(0, 2 * PLANE, drain_across, None)


def windows():
    for j in range(8):
        first = HEAD_DIM * j
        start = first // TILE * TILE
        stop = -(-(first + HEAD_DIM) // TILE) * TILE
        yield j, start, stop - start, first - start


def lanes(rows, width, offset):
    lane = lax.broadcasted_iota(jnp.int32, (rows, width), 1)
    return (lane >= offset) & (lane < offset + HEAD_DIM)


def nt(a, b):
    return lax.dot_general(a, b, (((1,), (1,)), ((), ())), preferred_element_type=jnp.float32)


def tn(a, b):
    return lax.dot_general(a, b, (((0,), (0,)), ((), ())), preferred_element_type=jnp.float32)


def nn(a, b):
    return jnp.dot(a, b, preferred_element_type=jnp.float32)


def each_group(body):
    lax.fori_loop(0, 2, lambda g, _: body(g, pl.multiple_of(HALF * g, TILE)), None)


def kept_lanes(ref, cols, value, keep):
    ref[:, cols] = jnp.where(keep, value, ref[:, cols])


def masked(value, keep):
    return jnp.where(keep, value, jnp.zeros((), value.dtype))


def project(s, r):
    x = r["x"][s].reshape(3 * RUN, WIDTH).astype(jnp.float32)
    inverse = lax.rsqrt(jnp.mean(x * x, axis=-1, keepdims=True) + 1e-05)
    r["normed"][...] = (x * inverse * r["scale"][s]).astype(jnp.bfloat16)
    r["inverse"][s] = jnp.broadcast_to(inverse[RUN : 2 * RUN], (RUN, TILE))
    for t, first in ((0, RUN), (1, 0), (2, 0)):

        def chunk(n, _):
            cols = pl.ds(pl.multiple_of(256 * n, 256), 256)
            r["qkv"][s, t, :, cols] = nn(r["normed"][first : first + 2 * RUN], r["w"][s, t, :, cols]).astype(
                jnp.bfloat16
            )

        lax.fori_loop(0, 5, chunk, None)


def attend(s, r):
    att = r["acc"].at[0]

    def group(g, base):
        for j, start, width, offset in windows():
            cols = pl.ds(base + start, width)
            keep = lanes(RUN, width, offset)
            query = masked(r["qkv"][s, 0, :RUN, cols], keep)
            scores = nt(r["qkv"][s, 1, :, cols], query) * (1.0 / math.sqrt(HEAD_DIM)) + r["bias"][...]
            highest = jnp.max(scores, axis=0, keepdims=True)
            exponent = jnp.exp(scores - highest)
            total = jnp.sum(exponent, axis=0, keepdims=True)
            soft = exponent / total
            r["soft"][s, 8 * g + j] = soft
            r["stats"][s, 8 * g + j, :, :RUN] = highest + jnp.log(total)
            kept_lanes(att, cols, tn(soft.astype(jnp.bfloat16), r["qkv"][s, 2, :, cols]), keep)

    each_group(group)
    return (r["x"][s, 1].astype(jnp.float32) + att[...]).astype(jnp.bfloat16)


def score_grads(s, r):
    def group(g, base):
        for j, start, width, offset in windows():
            cols = pl.ds(base + start, width)
            h = 8 * g + j
            flow = masked(r["flow"][s, 0, :, cols], lanes(RUN, width, offset))
            grad_soft = nt(r["qkv"][s, 2, :, cols], flow)
            soft = r["soft"][s, h]
            inner = jnp.sum(soft * grad_soft, axis=0, keepdims=True)
            r["stats"][2 + s, h, :, :RUN] = inner
            grad = (soft * (grad_soft - inner) * (1.0 / math.sqrt(HEAD_DIM))).astype(jnp.bfloat16)
            r["ds"][h] = grad
            r["softb"][h, :, :RUN] = soft[RUN:].astype(jnp.bfloat16)

    each_group(group)


def query_grads(s, r):
    def group(g, base):
        for j, start, width, offset in windows():
            cols = pl.ds(base + start, width)
            keep = lanes(RUN, width, offset)
            kept_lanes(r["acc"].at[0], cols, tn(r["ds"][8 * g + j], r["qkv"][s, 1, :, cols]), keep)

    each_group(group)
    r["gqkv"][0] = r["acc"][0].astype(jnp.bfloat16)


def next_soft(s, r):
    def group(g, base):
        for j, start, width, offset in windows():
            cols = pl.ds(base + start, width)
            query = masked(r["qkv"][s, 0, RUN:, cols], lanes(RUN, width, offset))
            scores = nt(r["qkv"][s, 1, RUN:, cols], query) * (1.0 / math.sqrt(HEAD_DIM)) + r["bias_next"][...]
            r["soft_next"][8 * g + j] = jnp.exp(scores - r["stats_next"][s, 8 * g + j, :, :RUN])

    each_group(group)


def key_grads(s, r):
    def group(g, base):
        for j, start, width, offset in windows():
            cols = pl.ds(base + start, width)
            h = 8 * g + j
            keep = lanes(RUN, width, offset)
            flow = masked(r["flow"][s, 1, :, cols], keep)
            grad_soft = nt(r["qkv"][s, 2, RUN:, cols], flow)
            soft = r["soft_next"][h]
            grad = (soft * (grad_soft - r["stats_next"][2 + s, h, :, :RUN]) * (1.0 / math.sqrt(HEAD_DIM))).astype(
                jnp.bfloat16
            )
            softb = soft.astype(jnp.bfloat16)
            values = nn(r["softb"][h, :, :RUN], r["flow"][s, 0, :, cols]) + nn(softb, r["flow"][s, 1, :, cols])
            keys = nn(r["ds"][h, RUN:], r["qkv"][s, 0, :RUN, cols]) + nn(grad, r["qkv"][s, 0, RUN:, cols])
            kept_lanes(r["acc"].at[0], cols, keys, keep)
            kept_lanes(r["acc"].at[1], cols, values, keep)

    each_group(group)
    r["gqkv"][1] = r["acc"][0].astype(jnp.bfloat16)
    r["gqkv"][2] = r["acc"][1].astype(jnp.bfloat16)


def back_project(s, r, kinds, add):
    def chunk(n, _):
        rows = pl.ds(pl.multiple_of(256 * n, 256), 256)
        total = nt(r["gqkv"][kinds[0]], r["w"][s, kinds[0], rows, :])
        for t in kinds[1:]:
            total = total + nt(r["gqkv"][t], r["w"][s, t, rows, :])
        if add:
            total = total + r["gn"][:, rows]
        r["gn"][:, rows] = total

    lax.fori_loop(0, 5, chunk, None)


def input_grad(s, r):
    x = r["x"][s, 1].astype(jnp.float32)
    inverse = r["inverse"][s][:, :1]
    grad = r["gn"][...]
    r["terms"][s : s + 1] = jnp.sum(grad * x * inverse, axis=0, keepdims=True)
    scaled = grad * r["scale"][s]
    moved = inverse * (scaled - x * inverse * inverse * jnp.mean(scaled * x, axis=-1, keepdims=True))
    return (r["flow"][s, 0].astype(jnp.float32) + moved).astype(jnp.bfloat16)


NAMES = (
    "w", "x", "flow", "normed", "inverse", "qkv", "soft", "softb", "soft_next", "ds", "gqkv", "acc", "gn",
    "terms", "stats", "stats_next", "scale", "result",
)
SHAPES = [
    pltpu.VMEM((2, 3, WIDTH, WIDTH), jnp.bfloat16),
    pltpu.VMEM((2, 3, RUN, WIDTH), jnp.bfloat16),
    pltpu.VMEM((2, 2, RUN, WIDTH), jnp.bfloat16),
    pltpu.VMEM((3 * RUN, WIDTH), jnp.bfloat16),
    pltpu.VMEM((2, RUN, TILE), jnp.float32),
    pltpu.VMEM((2, 3, 2 * RUN, WIDTH), jnp.bfloat16),
    pltpu.VMEM((2, HEADS, 2 * RUN, RUN), jnp.float32),
    pltpu.VMEM((HEADS, RUN, TILE), jnp.bfloat16),
    pltpu.VMEM((HEADS, RUN, RUN), jnp.float32),
    pltpu.VMEM((HEADS, 2 * RUN, RUN), jnp.bfloat16),
    pltpu.VMEM((3, RUN, WIDTH), jnp.bfloat16),
    pltpu.VMEM((2, RUN, WIDTH), jnp.float32),
    pltpu.VMEM((RUN, WIDTH), jnp.float32),
    pltpu.VMEM((8, WIDTH), jnp.float32),
    pltpu.VMEM((4, HEADS, 1, TILE), jnp.float32),
    pltpu.VMEM((4, HEADS, 1, TILE), jnp.float32),
    pltpu.VMEM((2, 1, WIDTH), jnp.float32),
    pltpu.VMEM((2, RUN, WIDTH), jnp.bfloat16),
]
REDUCE_SCRATCH = [
    pltpu.VMEM((LAYERS, 8, TILE), jnp.float32),
    pltpu.VMEM((LAYERS, 8, TILE), jnp.float32),
    pltpu.VMEM((2, 8, TILE), jnp.float32),
    pltpu.VMEM((2 * PLANE, 8, TILE), jnp.float32),
    pltpu.SemaphoreType.DMA((LAYERS,)),
    pltpu.SemaphoreType.DMA((LAYERS,)),
    pltpu.SemaphoreType.DMA((2 * PLANE,)),
    pltpu.SemaphoreType.DMA((2 * PLANE,)),
]


def whole_kernel(raw, tokens, upstream, bias, bias_next, gains, out, gain_out, *scratch):
    r = dict(zip(NAMES, scratch[: len(NAMES)]))
    r["bias"], r["bias_next"] = bias, bias_next
    hsend, hrecv, local = scratch[len(NAMES) : len(NAMES) + 3]
    rest = scratch[len(NAMES) + 3 :]
    core, dp, z, slot, _, _ = place()
    load = pltpu.make_async_copy(tokens.at[core], r["x"].at[0, 1], local.at[0])
    load.start()
    load_up = pltpu.make_async_copy(upstream, r["flow"].at[1, 0], local.at[1])
    load_up.start()
    load_gain = pltpu.make_async_copy(gains, r["scale"].at[core], local.at[2])
    load_gain.start()
    greet(core, dp, z, slot)
    after, before = (dp + 1) % DEVICES, (dp + DEVICES - 1) % DEVICES

    def hand(k, source, target, c, d):
        return pltpu.make_async_remote_copy(
            src_ref=source,
            dst_ref=target,
            send_sem=hsend.at[k],
            recv_sem=hrecv.at[k],
            device_id=(c, d),
            device_id_type=MESH,
        )

    x, flow, stats, stats_next = r["x"], r["flow"], r["stats"], r["stats_next"]
    hands = []
    for s in range(2):
        hands.append(hand(4 * s, x.at[s, 1], x.at[s, 0], core, after))
        hands.append(hand(4 * s + 1, x.at[s, 1], x.at[s, 2], core, before))
        hands.append(hand(4 * s + 2, flow.at[s, 0], flow.at[s, 1], core, before))
        hands.append(hand(4 * s + 3, stats.at[s], stats_next.at[s], core, before))
    for s in range(2):
        hands.append(hand(8 + s, stats.at[2 + s], stats_next.at[2 + s], core, before))
    hands.append(hand(10, gains, r["scale"].at[core], 1 - core, dp))
    hands.append(hand(11, r["result"].at[1 - core], out.at[0, core], 1 - core, dp))
    hands[10].start()
    load.wait()
    hands[0].start()
    hands[1].start()
    load_up.wait()
    hands[6].start()
    load_gain.wait()
    drain = gather_body(raw, r["w"], *rest[: len(GATHER_SCRATCH)])
    hands[10].wait_recv()
    hands[0].wait_recv()
    hands[1].wait_recv()
    project(0, r)
    x[1, 1] = attend(0, r)
    hands[4].start()
    hands[5].start()
    hands[3].start()
    hands[4].wait_recv()
    hands[5].wait_recv()
    project(1, r)
    r["result"][1] = attend(1, r)
    hands[7].start()
    hands[6].wait_recv()
    for s in (1, 0):
        score_grads(s, r)
        hands[8 + s].start()
        query_grads(s, r)
        hands[4 * s + 3].wait_recv()
        next_soft(s, r)
        back_project(s, r, (0,), False)
        hands[8 + s].wait_recv()
        if s == 0:
            hands[2].wait_recv()
        key_grads(s, r)
        back_project(s, r, (1, 2), True)
        if s == 1:
            flow[0, 0] = input_grad(1, r)
            hands[2].start()
        else:
            r["result"][0] = input_grad(0, r)
    hands[11].start()
    keep = pltpu.make_async_copy(r["result"].at[core], out.at[0, core], local.at[3])
    keep.start()
    reduce_body(r["terms"], gain_out, *rest[len(GATHER_SCRATCH) :])
    keep.wait()
    hands[11].wait_recv()
    for h in hands:
        h.wait_send()
    drain()


def shards(tokens, segment_ids, loss_mask, qkv_weight, gains, cotangent):
    core = lax.axis_index("phase")
    dp = lax.axis_index("dp")
    raw = jnp.transpose(qkv_weight.reshape(5, 3, WIDTH), (1, 0, 2)).reshape(15, WIDTH)
    raw = jnp.pad(raw, ((0, 1), (0, 0)))
    runs = [jnp.clip(dp + k, 0, DEVICES - 1) * RUN for k in (-1, 0, 1)]
    seg_prev, seg_own, seg_next = (
        lax.dynamic_slice(segment_ids, (core, start), (1, RUN))[0] for start in runs
    )
    position = jnp.arange(RUN)
    own_ok = (seg_own[None, :] == seg_own[:, None]) & (position[:, None] <= position[None, :])
    prev_ok = (seg_own[None, :] == seg_prev[:, None]) & (dp > 0)
    next_ok = (seg_next[None, :] == seg_own[:, None]) & (dp < DEVICES - 1)
    bias = jnp.where(jnp.concatenate([prev_ok, own_ok], axis=0), 0.0, NEVER).astype(jnp.float32)
    bias_next = jnp.where(next_ok, 0.0, NEVER).astype(jnp.float32)
    chosen = lax.dynamic_index_in_dim(cotangent, core, 0, keepdims=False)
    mask = lax.dynamic_index_in_dim(loss_mask, core, 0, keepdims=False)
    upstream = jnp.where(mask[:, None] == 1, chosen, jnp.zeros((), jnp.bfloat16))
    vmem = pl.BlockSpec(memory_space=pltpu.VMEM)
    hbm = pl.BlockSpec(memory_space=pl.ANY)
    boundary, row = pl.pallas_call(
        whole_kernel,
        out_shape=(
            jax.ShapeDtypeStruct((1, 2, RUN, WIDTH), jnp.bfloat16),
            jax.ShapeDtypeStruct((1, TILE), jnp.float32),
        ),
        in_specs=[vmem, hbm, hbm, vmem, vmem, vmem],
        out_specs=(hbm, vmem),
        scratch_shapes=SHAPES
        + [pltpu.SemaphoreType.DMA((12,)), pltpu.SemaphoreType.DMA((12,)), pltpu.SemaphoreType.DMA((4,))]
        + GATHER_SCRATCH
        + REDUCE_SCRATCH,
        compiler_params=pltpu.CompilerParams(
            collective_id=0, has_side_effects=True, vmem_limit_bytes=56 * 2**20
        ),
        name="sections",
    )(raw, tokens, upstream, bias, bias_next, gains)
    slot = dp % PLANE
    return boundary, lax.dynamic_slice(row, (0, 5 * slot), (1, 5))


def solution(mesh):
    in_specs = (
        P(None, "dp", None),
        P(),
        P(None, "dp"),
        P("phase", "dp", None),
        P("phase", None),
        P(None, "dp", None),
    )
    out_specs = (P("phase", None, "dp", None), P("phase", "dp"))
    return jax.shard_map(shards, mesh=mesh, in_specs=in_specs, out_specs=out_specs, check_vma=False)
```

time: 281 us -> 169 us (0.60)
  matrix products: 57.3 us -> 0 us
  starting transfers between devices: 24.9 us -> 0 us
  waiting for transfers between devices: 20.1 us -> 0 us
  other arithmetic: 10.1 us -> 2.91 us
  local copies, waits for them, and re-layouts: 12.3 us -> 5.33 us
  Pallas kernels: 153 us -> 159 us
    dot_general x22 -> x0, matrix products: 53.6 us -> none  [the longest x6 19 us: backward(): lax.dot_general(g.astype(jnp.bfloat16), w[t], (((1,), (1,)), ((), ())), p...]
    ppermute x6 -> x0, starting transfers between devices: 24.9 us -> none  [the longest x4 10.5 us: passed_along(): return lax.ppermute(x, axis, pairs)]
    ppermute x6 -> x0, waiting for transfers between devices: 20.1 us -> none  [the longest x4 20.1 us: passed_along(): return lax.ppermute(x, axis, pairs)]
    pallas_call x2 -> x1, Pallas kernels: 153 us -> 159 us  [shards(): pl.pallas_call(whole_kernel, out_shape=(jax.ShapeDtypeStruct((1, 2, RUN,...]
    sub x2 -> x0, matrix products: 3.7 us -> none  [forward(): exponent = jnp.exp(scores - jnp.max(scores, axis=-1, keepdims=True))]
  transfers between devices with their start and end apart: 6 -> 0, of which waited for: 4 -> 0; matrix products, arithmetic and copies ran while one was open for 10% -> 0% of each run, Pallas kernels for 55% -> 0%
where the time goes in v2:
time: 169 us; the launch traced here: 168 us
  Pallas kernels  159 us (94%)
  local copies, waits for them, and re-layouts  5.33 us (3%)
  other arithmetic  2.91 us (2%)
    pallas_call x1, Pallas kernels, shards(): pl.pallas_call(whole_kernel, out_shape=(jax.ShapeDtypeStruct((1, 2, RUN,...  159 us

profile of v2, /device:TPU:1, one launch (start us, length us, event | category | flops | bytes accessed | tf_op | source)
XLA Modules:
  0.0 168.2 jit_solution(11930333496516222089)
XLA Ops:
  0.6 0.0 copy-start
  0.7 0.9 dynamic-slice_bitcast_fusion
  1.5 0.7 compare_bitcast_fusion
  2.2 0.1 compare_and_fusion
  2.3 0.8 reshape.23
  3.2 0.6 pad.4.raw
  3.8 0.7 and_select_fusion.bias_next
  4.5 0.7 add_select_fusion.bias
  5.1 0.0 copy-done
  5.2 0.8 bitcast_select_fusion.upstream
  5.9 159.3 %sections.1 = (bf16[1,2,96,1280]{3,2,1,0:T(8,128)(2,1)}, f32[1,128]{1,0:T(1,128)}) custom-call(bf16[16,1280]{1,0:T(8,128)(2,1)} %pad.4.raw, bf16[2,96,1280]{2,1,0:T(8,128)(2,1)} %tokens.1, bf16[96,1280]{1,0:T(8,128)(2,1)} %bitcast_select_fusion.upstream, f32[192,96]{1,0:T(8,128)} %add_select_fusion.bias, f32[96,96]{1,0:T(8,128)} %and_select_fusion.bias_next, ...), custom_call_target="tpu_custom_call" | custom-call | tf_op jit(solution)/shard_map/sections/pallas_call | solution.py:641
  165.3 0.0 copy-start.1
  165.3 0.6 copy-done.1
  165.8 0.6 constant_dynamic-slice_fusion
  166.4 1.8 %copy.11 = bf16[1,2,96,1280]{3,2,1,0:T(8,128)(2,1)} copy(bf16[1,2,96,1280]{3,2,1,0:T(8,128)(2,1)} %get-tuple-element.13) | data formatting | bytes 983040
Async XLA Ops:
  0.6 4.5 %copy-start = (bf16[2,96,1280]{2,1,0:T(8,128)(2,1)S(1)}, bf16[2,96,1280]{2,1,0:T(8,128)(2,1)}, u32[]{:S(2)}) copy-start(bf16[2,96,1280]{2,1,0:T(8,128)(2,1)} %param.11) | copy-start | bytes 1474564
  165.3 0.6 copy-start.1

commit v3 on v2

--- a/solution.py
+++ b/solution.py
@@ -55,7 +55,7 @@
     pl.semaphore_wait(barrier, 2 * PLANE - 1 + LAYERS - 1 + 2)
 
 
-def gather_body(raw, w, sendbuf, stage, psend, pown, precv, zsend, zrecv, rsend, rrecv, ssend, srecv):
+def gather_body(prepare, raw, w, sendbuf, stage, psend, pown, precv, zsend, zrecv, rsend, rrecv, ssend, srecv):
     core, dp, z, slot, x, y = place()
     for c in range(2):
         for n in range(SIDE):
@@ -86,6 +86,7 @@
             piece(j).start()
 
     lax.fori_loop(0, 2 * PLANE, send_piece, None)
+    prepare()
     base = 5 * core
     my_tile = base + ring_place
     row = lax.broadcasted_iota(jnp.int32, (3 * PANEL, 16 * PLANE), 0)
@@ -268,73 +269,99 @@
 ]
 
 
-def reduce_body(terms, out, part, line, both, plane, lsend, lrecv, psend, precv):
+def reduce_body(terms, part, line, both, plane, lsend, lrecv, psend, precv):
     core, dp, z, slot, x, y = place()
-    for k in range(LAYERS):
-        part[k, 0:2, :] = jnp.concatenate(
-            [terms[0:2, PANEL * k : PANEL * (k + 1)], jnp.zeros((2, TILE - PANEL), jnp.float32)], axis=1
-        )
+    mine = 2 * slot + core
 
     def along(step):
         to = (z + step) % LAYERS
         return pltpu.make_async_remote_copy(
             src_ref=part.at[to],
             dst_ref=line.at[step],
-            send_sem=lsend.at[step],
-            recv_sem=lrecv.at[step],
+            send_sem=lsend,
+            recv_sem=lrecv,
             device_id=(core, PLANE * to + slot),
             device_id_type=MESH,
         )
-
-    def start_along(step, _):
-        along(step).start()
-
-    lax.fori_loop(1, LAYERS, start_along, None)
-    total = part[z, 0:2, :]
-    for step in range(1, LAYERS):
-        along(step).wait_recv()
-        total = total + line[step, 0:2, :]
-    both[0] = jnp.broadcast_to(total[0:1], (8, TILE))
-    both[1] = jnp.broadcast_to(total[1:2], (8, TILE))
-    mine = 2 * slot + core
 
     def across(j):
         return pltpu.make_async_remote_copy(
             src_ref=both.at[j % 2],
             dst_ref=plane.at[mine],
-            send_sem=psend.at[j],
-            recv_sem=precv.at[mine],
+            send_sem=psend,
+            recv_sem=precv,
             device_id=(j % 2, PLANE * z + j // 2),
             device_id_type=MESH,
         )
 
-    def start_across(j, _):
-        @pl.when(j != mine)
-        def _():
-            across(j).start()
-
-    lax.fori_loop(0, 2 * PLANE, start_across, None)
-    plane[mine] = both[core]
-
-    def arrive(j, _):
-        @pl.when(j != mine)
-        def _():
-            pltpu.make_async_copy(plane.at[j], plane.at[j], precv.at[j]).wait()
-
-    lax.fori_loop(0, 2 * PLANE, arrive, None)
-    out[...] = jnp.sum(plane[...], axis=0)[0:1]
-
-    def drain_along(step, _):
-        along(step).wait_send()
-
-    lax.fori_loop(1, LAYERS, drain_along, None)
-
-    def drain_across(j, _):
-        @pl.when(j != mine)
-        def _():
-            across(j).wait_send()
-
-    lax.fori_loop(0, 2 * PLANE, drain_across, None)
+    def begin():
+        for k in range(LAYERS):
+            part[k, 0:2, :PANEL] = terms[0:2, PANEL * k : PANEL * (k + 1)]
+
+        def start_along(step, _):
+            along(step).start()
+
+        lax.fori_loop(1, LAYERS, start_along, None)
+
+    def end():
+        batch = line.at[pl.ds(1, LAYERS - 1)]
+        pltpu.make_async_copy(batch, batch, lrecv).wait()
+        line[0, 0:2] = part[z, 0:2]
+        total = jnp.sum(line[:, 0:2, :], axis=0)
+        both[0, 0:1] = total[0:1]
+        both[1, 0:1] = total[1:2]
+
+        def start_across(j, _):
+            @pl.when(j != mine)
+            def _():
+                across(j).start()
+
+        lax.fori_loop(0, 2 * PLANE, start_across, None)
+        pltpu.make_async_copy(batch, batch, lsend).wait()
+        own = pltpu.make_async_copy(both.at[core], plane.at[mine], precv)
+        own.start()
+        pltpu.make_async_copy(plane, plane, precv).wait()
+        row = jnp.sum(plane[:, 0:1, :], axis=0)
+        others = plane.at[pl.ds(0, 2 * PLANE - 1)]
+        pltpu.make_async_copy(others, others, psend).wait()
+        return row, slot
+
+    return begin, end
+
+
+def eye(n):
+    return lax.broadcasted_iota(jnp.int32, (n, n), 0) == lax.broadcasted_iota(jnp.int32, (n, n), 1)
+
+
+def down(row):
+    return jnp.sum(jnp.where(eye(row.shape[1]), row, 0.0), axis=1, keepdims=True)
+
+
+def across_lanes(column):
+    return jnp.sum(jnp.where(eye(column.shape[0]), column, 0.0), axis=0, keepdims=True)
+
+
+def labels_of(segments, core, run):
+    first = RUN * run
+    start = jnp.minimum(first // TILE * TILE, RUN * DEVICES - 2 * TILE)
+    window = segments[pl.ds(core, 1), pl.ds(pl.multiple_of(start, TILE), 2 * TILE)].astype(jnp.float32)
+    row = lax.broadcasted_iota(jnp.int32, (RUN, 2 * TILE), 0)
+    lane = lax.broadcasted_iota(jnp.int32, (RUN, 2 * TILE), 1)
+    return jnp.sum(jnp.where(lane == row + (first - start), window, 0.0), axis=1, keepdims=True)
+
+
+def fill_biases(segments, bias, bias_next):
+    core, dp, _, _, _, _ = place()
+    own = labels_of(segments, core, dp)
+    prev = labels_of(segments, core, jnp.maximum(dp - 1, 0))
+    after = labels_of(segments, core, jnp.minimum(dp + 1, DEVICES - 1))
+    own_row, after_row = across_lanes(own), across_lanes(after)
+    key = lax.broadcasted_iota(jnp.int32, (RUN, RUN), 0)
+    query = lax.broadcasted_iota(jnp.int32, (RUN, RUN), 1)
+    never = jnp.float32(NEVER)
+    bias[:RUN] = jnp.where((prev == own_row) & (dp > 0), 0.0, never)
+    bias[RUN:] = jnp.where((own == own_row) & (key <= query), 0.0, never)
+    bias_next[...] = jnp.where((own == after_row) & (dp < DEVICES - 1), 0.0, never)
 
 
 def windows():
@@ -382,15 +409,15 @@
     for t, first in ((0, RUN), (1, 0), (2, 0)):
 
         def chunk(n, _):
-            cols = pl.ds(pl.multiple_of(256 * n, 256), 256)
+            cols = pl.ds(pl.multiple_of(HALF * n, TILE), HALF)
             r["qkv"][s, t, :, cols] = nn(r["normed"][first : first + 2 * RUN], r["w"][s, t, :, cols]).astype(
                 jnp.bfloat16
             )
 
-        lax.fori_loop(0, 5, chunk, None)
-
-
-def attend(s, r):
+        lax.fori_loop(0, 2, chunk, None)
+
+
+def attend(s, r, done):
     att = r["acc"].at[0]
 
     def group(g, base):
@@ -407,8 +434,9 @@
             r["stats"][s, 8 * g + j, :, :RUN] = highest + jnp.log(total)
             kept_lanes(att, cols, tn(soft.astype(jnp.bfloat16), r["qkv"][s, 2, :, cols]), keep)
 
-    each_group(group)
-    return (r["x"][s, 1].astype(jnp.float32) + att[...]).astype(jnp.bfloat16)
+    for g in range(2):
+        group(g, HALF * g)
+        done(g)
 
 
 def score_grads(s, r):
@@ -475,7 +503,7 @@
 
 def back_project(s, r, kinds, add):
     def chunk(n, _):
-        rows = pl.ds(pl.multiple_of(256 * n, 256), 256)
+        rows = pl.ds(pl.multiple_of(HALF * n, TILE), HALF)
         total = nt(r["gqkv"][kinds[0]], r["w"][s, kinds[0], rows, :])
         for t in kinds[1:]:
             total = total + nt(r["gqkv"][t], r["w"][s, t, rows, :])
@@ -483,14 +511,18 @@
             total = total + r["gn"][:, rows]
         r["gn"][:, rows] = total
 
-    lax.fori_loop(0, 5, chunk, None)
+    lax.fori_loop(0, 2, chunk, None)
+
+
+def gain_terms(s, r):
+    x = r["x"][s, 1].astype(jnp.float32)
+    r["terms"][s : s + 1] = jnp.sum(r["gn"][...] * x * r["inverse"][s][:, :1], axis=0, keepdims=True)
 
 
 def input_grad(s, r):
     x = r["x"][s, 1].astype(jnp.float32)
     inverse = r["inverse"][s][:, :1]
     grad = r["gn"][...]
-    r["terms"][s : s + 1] = jnp.sum(grad * x * inverse, axis=0, keepdims=True)
     scaled = grad * r["scale"][s]
     moved = inverse * (scaled - x * inverse * inverse * jnp.mean(scaled * x, axis=-1, keepdims=True))
     return (r["flow"][s, 0].astype(jnp.float32) + moved).astype(jnp.bfloat16)
@@ -498,7 +530,7 @@
 
 NAMES = (
     "w", "x", "flow", "normed", "inverse", "qkv", "soft", "softb", "soft_next", "ds", "gqkv", "acc", "gn",
-    "terms", "stats", "stats_next", "scale", "result",
+    "terms", "stats", "stats_next", "scale", "result", "bias", "bias_next", "raw",
 )
 SHAPES = [
     pltpu.VMEM((2, 3, WIDTH, WIDTH), jnp.bfloat16),
@@ -519,31 +551,36 @@
     pltpu.VMEM((4, HEADS, 1, TILE), jnp.float32),
     pltpu.VMEM((2, 1, WIDTH), jnp.float32),
     pltpu.VMEM((2, RUN, WIDTH), jnp.bfloat16),
+    pltpu.VMEM((2 * RUN, RUN), jnp.float32),
+    pltpu.VMEM((RUN, RUN), jnp.float32),
+    pltpu.VMEM((16, WIDTH), jnp.bfloat16),
 ]
 REDUCE_SCRATCH = [
     pltpu.VMEM((LAYERS, 8, TILE), jnp.float32),
     pltpu.VMEM((LAYERS, 8, TILE), jnp.float32),
     pltpu.VMEM((2, 8, TILE), jnp.float32),
     pltpu.VMEM((2 * PLANE, 8, TILE), jnp.float32),
-    pltpu.SemaphoreType.DMA((LAYERS,)),
-    pltpu.SemaphoreType.DMA((LAYERS,)),
-    pltpu.SemaphoreType.DMA((2 * PLANE,)),
-    pltpu.SemaphoreType.DMA((2 * PLANE,)),
+    pltpu.SemaphoreType.DMA,
+    pltpu.SemaphoreType.DMA,
+    pltpu.SemaphoreType.DMA,
+    pltpu.SemaphoreType.DMA,
 ]
 
 
-def whole_kernel(raw, tokens, upstream, bias, bias_next, gains, out, gain_out, *scratch):
+def whole_kernel(shard, tokens, segments, mask, cotangent, gains, out, gain_out, *scratch):
     r = dict(zip(NAMES, scratch[: len(NAMES)]))
-    r["bias"], r["bias_next"] = bias, bias_next
     hsend, hrecv, local = scratch[len(NAMES) : len(NAMES) + 3]
     rest = scratch[len(NAMES) + 3 :]
     core, dp, z, slot, _, _ = place()
     load = pltpu.make_async_copy(tokens.at[core], r["x"].at[0, 1], local.at[0])
     load.start()
-    load_up = pltpu.make_async_copy(upstream, r["flow"].at[1, 0], local.at[1])
+    load_up = pltpu.make_async_copy(cotangent.at[core], r["flow"].at[1, 0], local.at[1])
     load_up.start()
     load_gain = pltpu.make_async_copy(gains, r["scale"].at[core], local.at[2])
     load_gain.start()
+    wide = shard[0].astype(jnp.float32)
+    parts = [wide[:, WIDTH * t : WIDTH * (t + 1)] for t in range(3)]
+    r["raw"][...] = jnp.concatenate(parts + [jnp.zeros((1, WIDTH), jnp.float32)], axis=0).astype(jnp.bfloat16)
     greet(core, dp, z, slot)
     after, before = (dp + 1) % DEVICES, (dp + DEVICES - 1) % DEVICES
 
@@ -558,105 +595,110 @@
         )
 
     x, flow, stats, stats_next = r["x"], r["flow"], r["stats"], r["stats_next"]
-    hands = []
-    for s in range(2):
-        hands.append(hand(4 * s, x.at[s, 1], x.at[s, 0], core, after))
-        hands.append(hand(4 * s + 1, x.at[s, 1], x.at[s, 2], core, before))
-        hands.append(hand(4 * s + 2, flow.at[s, 0], flow.at[s, 1], core, before))
-        hands.append(hand(4 * s + 3, stats.at[s], stats_next.at[s], core, before))
-    for s in range(2):
-        hands.append(hand(8 + s, stats.at[2 + s], stats_next.at[2 + s], core, before))
-    hands.append(hand(10, gains, r["scale"].at[core], 1 - core, dp))
-    hands.append(hand(11, r["result"].at[1 - core], out.at[0, core], 1 - core, dp))
-    hands[10].start()
+    give_scale = hand(0, gains, r["scale"].at[core], 1 - core, dp)
+    give_result = hand(1, r["result"].at[1 - core], out.at[0, core], 1 - core, dp)
+    give_first = [hand(2, x.at[0, 1], x.at[0, 0], core, after), hand(3, x.at[0, 1], x.at[0, 2], core, before)]
+    give_flow = [hand(4 + s, flow.at[s, 0], flow.at[s, 1], core, before) for s in range(2)]
+    give_lse = [hand(6 + s, stats.at[s], stats_next.at[s], core, before) for s in range(2)]
+    give_inner = [hand(8 + s, stats.at[2 + s], stats_next.at[2 + s], core, before) for s in range(2)]
+    give_middle = []
+    for g in range(2):
+        cols = pl.ds(HALF * g, HALF)
+        give_middle.append(hand(10 + 2 * g, x.at[1, 1, :, cols], x.at[1, 0, :, cols], core, after))
+        give_middle.append(hand(11 + 2 * g, x.at[1, 1, :, cols], x.at[1, 2, :, cols], core, before))
+    give_scale.start()
     load.wait()
-    hands[0].start()
-    hands[1].start()
-    load_up.wait()
-    hands[6].start()
-    load_gain.wait()
-    drain = gather_body(raw, r["w"], *rest[: len(GATHER_SCRATCH)])
-    hands[10].wait_recv()
-    hands[0].wait_recv()
-    hands[1].wait_recv()
+    for h in give_first:
+        h.start()
+
+    def prepare():
+        load_up.wait()
+        chosen = down(mask[pl.ds(core, 1), :].astype(jnp.float32)) == 1.0
+        flow[1, 0] = jnp.where(chosen, flow[1, 0].astype(jnp.float32), 0.0).astype(jnp.bfloat16)
+        give_flow[1].start()
+        load_gain.wait()
+        fill_biases(segments, r["bias"], r["bias_next"])
+
+    drain = gather_body(prepare, r["raw"], r["w"], *rest[: len(GATHER_SCRATCH)])
+    begin, end = reduce_body(r["terms"], *rest[len(GATHER_SCRATCH) :])
+    give_scale.wait_recv()
+    for h in give_first:
+        h.wait_recv()
     project(0, r)
-    x[1, 1] = attend(0, r)
-    hands[4].start()
-    hands[5].start()
-    hands[3].start()
-    hands[4].wait_recv()
-    hands[5].wait_recv()
+
+    def middle(g):
+        cols = slice(HALF * g, HALF * (g + 1))
+        x[1, 1, :, cols] = (x[0, 1, :, cols].astype(jnp.float32) + r["acc"][0, :, cols]).astype(jnp.bfloat16)
+        give_middle[2 * g].start()
+        give_middle[2 * g + 1].start()
+
+    attend(0, r, middle)
+    give_lse[0].start()
+    drain()
+    for h in give_middle:
+        h.wait_recv()
     project(1, r)
-    r["result"][1] = attend(1, r)
-    hands[7].start()
-    hands[6].wait_recv()
+
+    def final(g):
+        cols = slice(HALF * g, HALF * (g + 1))
+        r["result"][1, :, cols] = (x[1, 1, :, cols].astype(jnp.float32) + r["acc"][0, :, cols]).astype(jnp.bfloat16)
+
+    attend(1, r, final)
+    give_lse[1].start()
+    give_flow[1].wait_recv()
     for s in (1, 0):
         score_grads(s, r)
-        hands[8 + s].start()
+        give_inner[s].start()
         query_grads(s, r)
-        hands[4 * s + 3].wait_recv()
+        give_lse[s].wait_recv()
         next_soft(s, r)
         back_project(s, r, (0,), False)
-        hands[8 + s].wait_recv()
+        give_inner[s].wait_recv()
         if s == 0:
-            hands[2].wait_recv()
+            give_flow[0].wait_recv()
         key_grads(s, r)
         back_project(s, r, (1, 2), True)
+        gain_terms(s, r)
         if s == 1:
             flow[0, 0] = input_grad(1, r)
-            hands[2].start()
+            give_flow[0].start()
         else:
+            begin()
             r["result"][0] = input_grad(0, r)
-    hands[11].start()
+    give_result.start()
     keep = pltpu.make_async_copy(r["result"].at[core], out.at[0, core], local.at[3])
     keep.start()
-    reduce_body(r["terms"], gain_out, *rest[len(GATHER_SCRATCH) :])
+    row, slot = end()
+    spread = down(row)
+    sub = lax.broadcasted_iota(jnp.int32, (TILE, TILE), 0)
+    lane = lax.broadcasted_iota(jnp.int32, (TILE, TILE), 1)
+    gain_out[...] = jnp.sum(jnp.where(sub == lane + 5 * slot, spread, 0.0), axis=0, keepdims=True)[:, :5]
     keep.wait()
-    hands[11].wait_recv()
-    for h in hands:
+    give_result.wait_recv()
+    for h in [give_scale, give_result] + give_first + give_flow + give_lse + give_inner + give_middle:
         h.wait_send()
-    drain()
 
 
 def shards(tokens, segment_ids, loss_mask, qkv_weight, gains, cotangent):
-    core = lax.axis_index("phase")
-    dp = lax.axis_index("dp")
-    raw = jnp.transpose(qkv_weight.reshape(5, 3, WIDTH), (1, 0, 2)).reshape(15, WIDTH)
-    raw = jnp.pad(raw, ((0, 1), (0, 0)))
-    runs = [jnp.clip(dp + k, 0, DEVICES - 1) * RUN for k in (-1, 0, 1)]
-    seg_prev, seg_own, seg_next = (
-        lax.dynamic_slice(segment_ids, (core, start), (1, RUN))[0] for start in runs
-    )
-    position = jnp.arange(RUN)
-    own_ok = (seg_own[None, :] == seg_own[:, None]) & (position[:, None] <= position[None, :])
-    prev_ok = (seg_own[None, :] == seg_prev[:, None]) & (dp > 0)
-    next_ok = (seg_next[None, :] == seg_own[:, None]) & (dp < DEVICES - 1)
-    bias = jnp.where(jnp.concatenate([prev_ok, own_ok], axis=0), 0.0, NEVER).astype(jnp.float32)
-    bias_next = jnp.where(next_ok, 0.0, NEVER).astype(jnp.float32)
-    chosen = lax.dynamic_index_in_dim(cotangent, core, 0, keepdims=False)
-    mask = lax.dynamic_index_in_dim(loss_mask, core, 0, keepdims=False)
-    upstream = jnp.where(mask[:, None] == 1, chosen, jnp.zeros((), jnp.bfloat16))
     vmem = pl.BlockSpec(memory_space=pltpu.VMEM)
     hbm = pl.BlockSpec(memory_space=pl.ANY)
-    boundary, row = pl.pallas_call(
+    return pl.pallas_call(
         whole_kernel,
         out_shape=(
             jax.ShapeDtypeStruct((1, 2, RUN, WIDTH), jnp.bfloat16),
-            jax.ShapeDtypeStruct((1, TILE), jnp.float32),
+            jax.ShapeDtypeStruct((1, 5), jnp.float32),
         ),
-        in_specs=[vmem, hbm, hbm, vmem, vmem, vmem],
+        in_specs=[vmem, hbm, vmem, vmem, hbm, vmem],
         out_specs=(hbm, vmem),
         scratch_shapes=SHAPES
-        + [pltpu.SemaphoreType.DMA((12,)), pltpu.SemaphoreType.DMA((12,)), pltpu.SemaphoreType.DMA((4,))]
+        + [pltpu.SemaphoreType.DMA((14,)), pltpu.SemaphoreType.DMA((14,)), pltpu.SemaphoreType.DMA((4,))]
         + GATHER_SCRATCH
         + REDUCE_SCRATCH,
         compiler_params=pltpu.CompilerParams(
             collective_id=0, has_side_effects=True, vmem_limit_bytes=56 * 2**20
         ),
         name="sections",
-    )(raw, tokens, upstream, bias, bias_next, gains)
-    slot = dp % PLANE
-    return boundary, lax.dynamic_slice(row, (0, 5 * slot), (1, 5))
+    )(qkv_weight, tokens, segment_ids, loss_mask, cotangent, gains)
 
 
 def solution(mesh):

time: 169 us -> 153 us (0.905)
  Pallas kernels: 159 us -> 150 us
  local copies, waits for them, and re-layouts: 5.33 us -> 2.36 us
  other arithmetic: 2.91 us -> 0 us
    pallas_call x1, Pallas kernels: 159 us -> 150 us  [shards(): pl.pallas_call(whole_kernel, out_shape=(jax.ShapeDtypeStruct((1, 2, RUN,...]
    select_n x3 -> x0, other arithmetic: 2.13 us -> none  [the longest x1 0.78 us: shards(): jnp.where(mask[:, None] == 1, chosen, jnp.zeros((), jnp.bfloat16))]
where the time goes in v3:
time: 153 us
  Pallas kernels  150 us (98%)
  local copies, waits for them, and re-layouts  2.36 us (2%)
    pallas_call x1, Pallas kernels, shards(): pl.pallas_call(whole_kernel, out_shape=(jax.ShapeDtypeStruct((1, 2, RUN,...  150 us

profile of v3, /device:TPU:1, one launch (start us, length us, event | category | flops | bytes accessed | tf_op | source)
XLA Modules:
  0.0 153.0 jit_solution(14841485150954277423)
XLA Ops:
  0.6 150.0 %sections.1 = (bf16[1,2,96,1280]{3,2,1,0:T(8,128)(2,1)}, f32[1,5]{1,0:T(1,128)}) custom-call(bf16[1,5,3840]{2,1,0:T(8,128)(2,1)} %shard.1, bf16[2,96,1280]{2,1,0:T(8,128)(2,1)} %tokens.1, s32[2,24576]{1,0:T(2,128)} %segments.1, s32[2,96]{1,0:T(2,128)} %mask.1, bf16[2,96,1280]{2,1,0:T(8,128)(2,1)} %cotangent.1, f32[1,1280]{1,0:T(1,128)} %gains.1), custom_call_target="tpu_custom_call" | custom-call | tf_op jit(solution)/shard_map/sections/pallas_call | solution.py:685
  150.7 0.0 copy-start
  150.7 1.8 %copy.10 = bf16[1,2,96,1280]{3,2,1,0:T(8,128)(2,1)} copy(bf16[1,2,96,1280]{3,2,1,0:T(8,128)(2,1)} %get-tuple-element.4) | data formatting | bytes 983040
  152.5 0.0 copy-done
  152.5 0.5 copy.11
Async XLA Ops:
  150.7 1.9 %copy-start = (f32[1,5]{1,0:T(1,128)S(1)}, f32[1,5]{1,0:T(1,128)}, u32[]{:S(2)}) copy-start(f32[1,5]{1,0:T(1,128)} %get-tuple-element.5) | copy-start | bytes 64

commit v4 on v3

--- a/solution.py
+++ b/solution.py
@@ -18,19 +18,21 @@
 PANEL = 80
 TILE = 128
 HALF = 640
-RING_LAG = 4
-CHIP_LAG = 8
+LEAD = 0
+RING_LAG = 1
+CHIP_LAG = 3
 DEVICES = 256
 NEVER = -1e30
+PIECES = ((0, 384), (384, 256), (640, 384), (1024, 256))
 MESH = pl.DeviceIdType.MESH
 
 
 def place():
     core = lax.axis_index("phase")
     dp = lax.axis_index("dp")
-    z = dp // PLANE
-    slot = dp % PLANE
-    return core, dp, z, slot, slot // SIDE, slot % SIDE
+    z = lax.div(dp, PLANE)
+    slot = lax.rem(dp, PLANE)
+    return core, dp, z, slot, lax.div(slot, SIDE), lax.rem(slot, SIDE)
 
 
 def greet(core, dp, z, slot):
@@ -55,7 +57,7 @@
     pl.semaphore_wait(barrier, 2 * PLANE - 1 + LAYERS - 1 + 2)
 
 
-def gather_body(prepare, raw, w, sendbuf, stage, psend, pown, precv, zsend, zrecv, rsend, rrecv, ssend, srecv):
+def gather_body(prepare, fill, raw, w, sendbuf, stage, psend, pown, precv, zsend, zrecv, rsend, rrecv, ssend, srecv):
     core, dp, z, slot, x, y = place()
     for c in range(2):
         for n in range(SIDE):
@@ -86,7 +88,6 @@
             piece(j).start()
 
     lax.fori_loop(0, 2 * PLANE, send_piece, None)
-    prepare()
     base = 5 * core
     my_tile = base + ring_place
     row = lax.broadcasted_iota(jnp.int32, (3 * PANEL, 16 * PLANE), 0)
@@ -95,7 +96,7 @@
     wanted = (within // 5) * 16 + (row // PANEL) * 5 + within % 5
     select = (column == wanted).astype(jnp.float32).astype(jnp.bfloat16)
     rows = pl.ds(pl.multiple_of(PANEL * z, 16), PANEL)
-    for s in range(2):
+    def retile(s):
         pltpu.make_async_copy(stage.at[s], stage.at[s], precv.at[s]).wait()
         panel = jnp.dot(
             select, stage[s].reshape(16 * PLANE, 2 * TILE), preferred_element_type=jnp.float32
@@ -113,8 +114,6 @@
         def _():
             piece(j).wait_send()
 
-    lax.fori_loop(0, 2 * PLANE, drain_piece, None)
-
     def region(s, panel, tile, width=TILE):
         return w.at[
             s,
@@ -123,135 +122,157 @@
             pl.ds(pl.multiple_of(TILE * tile, TILE), width),
         ]
 
-    def tile_of(kind):
-        return my_tile if kind == 0 else base + 4
+    def wrapped(value, size):
+        return lax.rem(value, size)
 
     def panel_of(q):
-        k = (q + 1) // 2
-        sign = jnp.where(q % 2 == 1, -1, 1)
-        return (z + sign * k + LAYERS) % LAYERS
-
-    def z_copy(s, kind, panel, upward):
-        to = (z + jnp.where(upward == 1, 1, LAYERS - 1)) % LAYERS
-        piece_ref = region(s, panel, tile_of(kind))
+        k = lax.div(q + 1, 2)
+        return wrapped(z + LAYERS + (1 - 2 * lax.rem(q, 2)) * k, LAYERS)
+
+    line_devices = [PLANE * wrapped(z + LAYERS + move, LAYERS) + slot for move in (-1, 1)]
+    ring_steps = [wrapped(ring_place + step, SIDE) for step in range(SIDE)]
+    ring_tiles = [base + moved for moved in ring_steps]
+    ring_devices = [
+        PLANE * z + jnp.where(core == 0, SIDE * x + moved, SIDE * moved + y) for moved in ring_steps
+    ]
+    tiles = (my_tile, base + 4)
+
+    def z_copy(s, kind, panel, q, to):
+        piece_ref = region(s, panel, tiles[kind])
         return pltpu.make_async_remote_copy(
             src_ref=piece_ref,
             dst_ref=piece_ref,
-            send_sem=zsend.at[s, kind, upward, panel],
-            recv_sem=zrecv.at[s, kind, panel],
-            device_id=(core, PLANE * to + slot),
+            send_sem=zsend.at[s, kind, q],
+            recv_sem=zrecv.at[s, kind, q],
+            device_id=(core, to),
             device_id_type=MESH,
         )
 
-    def ring_device(step):
-        moved = (ring_place + step) % SIDE
-        return PLANE * z + jnp.where(core == 0, SIDE * x + moved, SIDE * moved + y)
-
-    def ring_tile(step):
-        return base + (ring_place + step) % SIDE
-
-    def ring_copy(s, panel, tile, step, way):
+    def ring_copy(s, panel, q, tile, to, way):
         piece_ref = region(s, panel, tile)
         return pltpu.make_async_remote_copy(
             src_ref=piece_ref,
             dst_ref=piece_ref,
-            send_sem=rsend.at[s, panel, way],
-            recv_sem=rrecv.at[s, panel, way],
-            device_id=(core, ring_device(step)),
+            send_sem=rsend.at[s, q, way],
+            recv_sem=rrecv.at[s, q, way],
+            device_id=(core, to),
             device_id_type=MESH,
         )
 
-    def passed_on(s, panel):
-        even = panel % 2 == 0
-        tile = jnp.where(even, ring_tile(SIDE - 1), ring_tile(1))
-        return ring_copy(s, panel, tile, jnp.where(even, 1, SIDE - 1), 2)
-
-    def sibling_copy(s, panel):
+    def sibling_copy(s, panel, q):
         piece_ref = region(s, panel, base, HALF)
         return pltpu.make_async_remote_copy(
             src_ref=piece_ref,
             dst_ref=piece_ref,
-            send_sem=ssend.at[s, panel],
-            recv_sem=srecv.at[s, panel],
+            send_sem=ssend.at[s, q],
+            recv_sem=srecv.at[s, q],
             device_id=(1 - core, dp),
             device_id_type=MESH,
         )
 
+    def start_rings(s, panel, q):
+        ring_copy(s, panel, q, my_tile, ring_devices[1], 0).start()
+        ring_copy(s, panel, q, my_tile, ring_devices[3], 1).start()
+
+    def begin(s):
+        for kind in range(2):
+            for way in range(2):
+                z_copy(s, kind, z, 1 + way, line_devices[1 - way]).start()
+        start_rings(s, z, 0)
+
+    for s in range(2):
+        retile(s)
+        if LEAD == 0 or s == 0:
+            begin(s)
+    prepare()
+
     def step(i, _):
-        @pl.when(i < 32)
-        def _():
-            s, q = i % 2, i // 2
-            panel = panel_of(q)
-            upward = q % 2
-
-            @pl.when(q == 0)
+        for s in range(2):
+            q = i - LEAD * s
+
+            if LEAD > 0 and s == 1:
+
+                @pl.when(q == 0)
+                def _():
+                    begin(1)
+
+            @pl.when((q >= 1) & (q < 16))
             def _():
-                for kind in range(2):
-                    for way in range(2):
-                        z_copy(s, kind, panel, way).start()
-
-            @pl.when(q > 0)
-            def _():
-                z_copy(s, 0, panel, upward).wait_recv()
+                panel = panel_of(q)
+                to = jnp.where(lax.rem(q, 2) == 1, line_devices[1], line_devices[0])
+                z_copy(s, 0, panel, q, to).wait_recv()
 
                 @pl.when(q < 14)
                 def _():
-                    z_copy(s, 0, panel, upward).start()
-
-                z_copy(s, 1, panel, upward).wait_recv()
+                    z_copy(s, 0, panel, q + 2, to).start()
+
+                z_copy(s, 1, panel, q, to).wait_recv()
 
                 @pl.when((q < 13) | (q == 14))
                 def _():
-                    z_copy(s, 1, panel, upward).start()
-
-            ring_copy(s, panel, my_tile, 1, 0).start()
-            ring_copy(s, panel, my_tile, SIDE - 1, 1).start()
-
-        @pl.when((i >= RING_LAG) & (i < 32 + RING_LAG))
-        def _():
-            s, q = (i - RING_LAG) % 2, (i - RING_LAG) // 2
-            panel = panel_of(q)
-            ring_copy(s, panel, ring_tile(SIDE - 1), 1, 0).wait_recv()
-            ring_copy(s, panel, ring_tile(1), 1, 1).wait_recv()
-            passed_on(s, panel).start()
-
-        @pl.when(i >= CHIP_LAG)
-        def _():
-            s, q = (i - CHIP_LAG) % 2, (i - CHIP_LAG) // 2
-            panel = panel_of(q)
-            ring_copy(s, panel, ring_tile(2), 1, 2).wait_recv()
-            sibling_copy(s, panel).start()
-
-    lax.fori_loop(0, 32 + CHIP_LAG, step, None)
-
-    def arrive(i, _):
-        sibling_copy(i // 16, i % 16).wait_recv()
-
-    lax.fori_loop(0, 32, arrive, None)
-
-    def finish(i, _):
-        s, q = i // 16, i % 16
+                    z_copy(s, 1, panel, q + 2 - lax.div(q, 14), to).start()
+
+                start_rings(s, panel, q)
+
+        for s in range(2):
+            passing = i - LEAD * s - RING_LAG
+
+            @pl.when((passing >= 0) & (passing < 16))
+            def _():
+                panel = panel_of(passing)
+                even = lax.rem(panel, 2) == 0
+                tile = jnp.where(even, ring_tiles[3], ring_tiles[1])
+                to = jnp.where(even, ring_devices[1], ring_devices[3])
+                ring_copy(s, panel, passing, ring_tiles[3], to, 0).wait_recv()
+                ring_copy(s, panel, passing, ring_tiles[1], to, 1).wait_recv()
+                ring_copy(s, panel, passing, tile, to, 2).start()
+
+        for s in range(2):
+            complete = i - LEAD * s - CHIP_LAG
+
+            @pl.when((complete >= 0) & (complete < 16))
+            def _():
+                panel = panel_of(complete)
+                ring_copy(s, panel, complete, ring_tiles[2], dp, 2).wait_recv()
+                sibling_copy(s, panel, complete).start()
+
+    def arrived(s):
+        def one(q, _):
+            sibling_copy(s, panel_of(q), q).wait_recv()
+
+        lax.fori_loop(0, 16, one, None)
+
+    lax.fori_loop(1, 16 + LEAD, step, None)
+    if CHIP_LAG <= LEAD:
+        arrived(0)
+        fill(0)
+        for n in range(CHIP_LAG):
+            lax.fori_loop(16 + LEAD + n, 17 + LEAD + n, step, None)
+            fill(n + 1)
+    else:
+        lax.fori_loop(16 + LEAD, 16 + LEAD + CHIP_LAG, step, None)
+        arrived(0)
+        for n in range(3):
+            fill(n)
+    arrived(1)
+
+    def finish(q, _):
         panel = panel_of(q)
-        sibling_copy(s, panel).wait_send()
-
-        for way in range(3):
-            ring_copy(s, panel, my_tile, 1, way).wait_send()
-
-        @pl.when(q == 0)
-        def _():
+        for s in range(2):
+            sibling_copy(s, panel, q).wait_send()
+            for way in range(3):
+                ring_copy(s, panel, q, my_tile, dp, way).wait_send()
             for kind in range(2):
-                for way in range(2):
-                    z_copy(s, kind, panel, way).wait_send()
-
-        @pl.when((q > 0) & (q < 14))
-        def _():
-            z_copy(s, 0, panel, q % 2).wait_send()
-
-        @pl.when(((q > 0) & (q < 13)) | (q == 14))
-        def _():
-            z_copy(s, 1, panel, q % 2).wait_send()
-
-    return lambda: lax.fori_loop(0, 32, finish, None)
+
+                @pl.when(q > 0)
+                def _():
+                    z_copy(s, kind, panel, q, dp).wait_send()
+
+    def drain():
+        lax.fori_loop(0, 2 * PLANE, drain_piece, None)
+        lax.fori_loop(0, 16, finish, None)
+
+    return drain
 
 
 GATHER_SCRATCH = [
@@ -260,7 +281,7 @@
     pltpu.SemaphoreType.DMA((2 * PLANE,)),
     pltpu.SemaphoreType.DMA,
     pltpu.SemaphoreType.DMA((2,)),
-    pltpu.SemaphoreType.DMA((2, 2, 2, LAYERS)),
+    pltpu.SemaphoreType.DMA((2, 2, LAYERS)),
     pltpu.SemaphoreType.DMA((2, 2, LAYERS)),
     pltpu.SemaphoreType.DMA((2, LAYERS, 3)),
     pltpu.SemaphoreType.DMA((2, LAYERS, 3)),
@@ -401,20 +422,24 @@
     return jnp.where(keep, value, jnp.zeros((), value.dtype))
 
 
-def project(s, r):
+def normalize(s, r):
     x = r["x"][s].reshape(3 * RUN, WIDTH).astype(jnp.float32)
     inverse = lax.rsqrt(jnp.mean(x * x, axis=-1, keepdims=True) + 1e-05)
     r["normed"][...] = (x * inverse * r["scale"][s]).astype(jnp.bfloat16)
     r["inverse"][s] = jnp.broadcast_to(inverse[RUN : 2 * RUN], (RUN, TILE))
-    for t, first in ((0, RUN), (1, 0), (2, 0)):
+
+
+def project(s, r, kinds=(0, 1, 2)):
+    for t in kinds:
+        first = RUN if t == 0 else 0
 
         def chunk(n, _):
-            cols = pl.ds(pl.multiple_of(HALF * n, TILE), HALF)
+            cols = pl.ds(0, WIDTH)
             r["qkv"][s, t, :, cols] = nn(r["normed"][first : first + 2 * RUN], r["w"][s, t, :, cols]).astype(
                 jnp.bfloat16
             )
 
-        lax.fori_loop(0, 2, chunk, None)
+        chunk(0, None)
 
 
 def attend(s, r, done):
@@ -433,10 +458,11 @@
             r["soft"][s, 8 * g + j] = soft
             r["stats"][s, 8 * g + j, :, :RUN] = highest + jnp.log(total)
             kept_lanes(att, cols, tn(soft.astype(jnp.bfloat16), r["qkv"][s, 2, :, cols]), keep)
+            if j in (4, 7):
+                done(2 * g + j // 7)
 
     for g in range(2):
         group(g, HALF * g)
-        done(g)
 
 
 def score_grads(s, r):
@@ -503,7 +529,7 @@
 
 def back_project(s, r, kinds, add):
     def chunk(n, _):
-        rows = pl.ds(pl.multiple_of(HALF * n, TILE), HALF)
+        rows = pl.ds(0, WIDTH)
         total = nt(r["gqkv"][kinds[0]], r["w"][s, kinds[0], rows, :])
         for t in kinds[1:]:
             total = total + nt(r["gqkv"][t], r["w"][s, t, rows, :])
@@ -511,7 +537,7 @@
             total = total + r["gn"][:, rows]
         r["gn"][:, rows] = total
 
-    lax.fori_loop(0, 2, chunk, None)
+    chunk(0, None)
 
 
 def gain_terms(s, r):
@@ -567,7 +593,7 @@
 ]
 
 
-def whole_kernel(shard, tokens, segments, mask, cotangent, gains, out, gain_out, *scratch):
+def whole_kernel(shard, tokens, segments, mask, cotangent, gains, kept_out, got_out, gain_out, *scratch):
     r = dict(zip(NAMES, scratch[: len(NAMES)]))
     hsend, hrecv, local = scratch[len(NAMES) : len(NAMES) + 3]
     rest = scratch[len(NAMES) + 3 :]
@@ -596,22 +622,22 @@
 
     x, flow, stats, stats_next = r["x"], r["flow"], r["stats"], r["stats_next"]
     give_scale = hand(0, gains, r["scale"].at[core], 1 - core, dp)
-    give_result = hand(1, r["result"].at[1 - core], out.at[0, core], 1 - core, dp)
+    give_result = hand(1, r["result"].at[1 - core], got_out, 1 - core, dp)
     give_first = [hand(2, x.at[0, 1], x.at[0, 0], core, after), hand(3, x.at[0, 1], x.at[0, 2], core, before)]
     give_flow = [hand(4 + s, flow.at[s, 0], flow.at[s, 1], core, before) for s in range(2)]
     give_lse = [hand(6 + s, stats.at[s], stats_next.at[s], core, before) for s in range(2)]
     give_inner = [hand(8 + s, stats.at[2 + s], stats_next.at[2 + s], core, before) for s in range(2)]
     give_middle = []
-    for g in range(2):
-        cols = pl.ds(HALF * g, HALF)
-        give_middle.append(hand(10 + 2 * g, x.at[1, 1, :, cols], x.at[1, 0, :, cols], core, after))
-        give_middle.append(hand(11 + 2 * g, x.at[1, 1, :, cols], x.at[1, 2, :, cols], core, before))
-    give_scale.start()
-    load.wait()
-    for h in give_first:
-        h.start()
+    for p, (start, width) in enumerate(PIECES):
+        cols = pl.ds(start, width)
+        give_middle.append(hand(10 + 2 * p, x.at[1, 1, :, cols], x.at[1, 0, :, cols], core, after))
+        give_middle.append(hand(11 + 2 * p, x.at[1, 1, :, cols], x.at[1, 2, :, cols], core, before))
 
     def prepare():
+        give_scale.start()
+        load.wait()
+        for h in give_first:
+            h.start()
         load_up.wait()
         chosen = down(mask[pl.ds(core, 1), :].astype(jnp.float32)) == 1.0
         flow[1, 0] = jnp.where(chosen, flow[1, 0].astype(jnp.float32), 0.0).astype(jnp.bfloat16)
@@ -619,15 +645,19 @@
         load_gain.wait()
         fill_biases(segments, r["bias"], r["bias_next"])
 
-    drain = gather_body(prepare, r["raw"], r["w"], *rest[: len(GATHER_SCRATCH)])
+    def fill(n):
+        if n == 0:
+            give_scale.wait_recv()
+            for h in give_first:
+                h.wait_recv()
+            normalize(0, r)
+        project(0, r, (n,))
+
+    drain = gather_body(prepare, fill, r["raw"], r["w"], *rest[: len(GATHER_SCRATCH)])
     begin, end = reduce_body(r["terms"], *rest[len(GATHER_SCRATCH) :])
-    give_scale.wait_recv()
-    for h in give_first:
-        h.wait_recv()
-    project(0, r)
 
     def middle(g):
-        cols = slice(HALF * g, HALF * (g + 1))
+        cols = slice(PIECES[g][0], sum(PIECES[g]))
         x[1, 1, :, cols] = (x[0, 1, :, cols].astype(jnp.float32) + r["acc"][0, :, cols]).astype(jnp.bfloat16)
         give_middle[2 * g].start()
         give_middle[2 * g + 1].start()
@@ -637,10 +667,11 @@
     drain()
     for h in give_middle:
         h.wait_recv()
+    normalize(1, r)
     project(1, r)
 
     def final(g):
-        cols = slice(HALF * g, HALF * (g + 1))
+        cols = slice(PIECES[g][0], sum(PIECES[g]))
         r["result"][1, :, cols] = (x[1, 1, :, cols].astype(jnp.float32) + r["acc"][0, :, cols]).astype(jnp.bfloat16)
 
     attend(1, r, final)
@@ -666,7 +697,7 @@
             begin()
             r["result"][0] = input_grad(0, r)
     give_result.start()
-    keep = pltpu.make_async_copy(r["result"].at[core], out.at[0, core], local.at[3])
+    keep = pltpu.make_async_copy(r["result"].at[core], kept_out, local.at[3])
     keep.start()
     row, slot = end()
     spread = down(row)
@@ -682,16 +713,17 @@
 def shards(tokens, segment_ids, loss_mask, qkv_weight, gains, cotangent):
     vmem = pl.BlockSpec(memory_space=pltpu.VMEM)
     hbm = pl.BlockSpec(memory_space=pl.ANY)
-    return pl.pallas_call(
+    kept, got, gain_grad = pl.pallas_call(
         whole_kernel,
         out_shape=(
-            jax.ShapeDtypeStruct((1, 2, RUN, WIDTH), jnp.bfloat16),
+            jax.ShapeDtypeStruct((RUN, WIDTH), jnp.bfloat16),
+            jax.ShapeDtypeStruct((RUN, WIDTH), jnp.bfloat16),
             jax.ShapeDtypeStruct((1, 5), jnp.float32),
         ),
         in_specs=[vmem, hbm, vmem, vmem, hbm, vmem],
-        out_specs=(hbm, vmem),
+        out_specs=(hbm, hbm, vmem),
         scratch_shapes=SHAPES
-        + [pltpu.SemaphoreType.DMA((14,)), pltpu.SemaphoreType.DMA((14,)), pltpu.SemaphoreType.DMA((4,))]
+        + [pltpu.SemaphoreType.DMA((18,)), pltpu.SemaphoreType.DMA((18,)), pltpu.SemaphoreType.DMA((4,))]
         + GATHER_SCRATCH
         + REDUCE_SCRATCH,
         compiler_params=pltpu.CompilerParams(
@@ -699,6 +731,9 @@
         ),
         name="sections",
     )(qkv_weight, tokens, segment_ids, loss_mask, cotangent, gains)
+    own_first = lax.axis_index("phase") == 0
+    pair = [jnp.where(own_first, kept, got), jnp.where(own_first, got, kept)]
+    return jnp.stack(pair)[None], gain_grad
 
 
 def solution(mesh):

time: 153 us -> 147 us (0.961)
  Pallas kernels: 150 us -> 144 us
  other arithmetic: 0 us -> 1.93 us
  local copies, waits for them, and re-layouts: 2.36 us -> 0.51 us
    pallas_call x1, Pallas kernels: 150 us -> 144 us  [shards(): pl.pallas_call(whole_kernel, out_shape=(jax.ShapeDtypeStruct((RUN, WIDTH)...]
    unnamed x4 -> x3, local copies, waits for them, and re-layouts: 2.36 us -> 0.51 us
where the time goes in v4:
time: 147 us
  Pallas kernels  144 us (98%)
  other arithmetic  1.93 us (1%)
    pallas_call x1, Pallas kernels, shards(): pl.pallas_call(whole_kernel, out_shape=(jax.ShapeDtypeStruct((RUN, WIDTH)...  144 us

profile of v4, /device:TPU:1, one launch (start us, length us, event | category | flops | bytes accessed | tf_op | source)
XLA Modules:
  0.0 147.1 jit_solution(6326314288548662517)
XLA Ops:
  0.6 144.0 %sections.1 = (bf16[96,1280]{1,0:T(8,128)(2,1)}, bf16[96,1280]{1,0:T(8,128)(2,1)}, f32[1,5]{1,0:T(1,128)}) custom-call(bf16[1,5,3840]{2,1,0:T(8,128)(2,1)} %shard.1, bf16[2,96,1280]{2,1,0:T(8,128)(2,1)} %tokens.1, s32[2,24576]{1,0:T(2,128)} %segments.1, s32[2,96]{1,0:T(2,128)} %mask.1, bf16[2,96,1280]{2,1,0:T(8,128)(2,1)} %cotangent.1, f32[1,1280]{1,0:T(1,128)} %gains.1), custom_call_target="tpu_custom_call" | custom-call | tf_op jit(solution)/shard_map/sections/pallas_call | solution.py:716
  144.7 1.1 select_bitcast_fusion.1
  145.8 0.0 copy-start
  145.8 0.8 maximum_bitcast_fusion
  146.6 0.0 copy-done
  146.6 0.5 copy.9
Async XLA Ops:
  145.8 0.8 copy-start
